TPU v7x, 256 devices: a whole 4x4x8 slice. The times are simulated.
256 devices in a mesh: grp: 4 (over x_hi, core), vocab: 64 (over z, x_lo, y).
Axes of the slice: x: 4 (x_hi: 2, x_lo: 2; x = x_hi * 2 + x_lo), y: 4, z: 8, core: 2. Of those that a mesh axis runs over, the one named last changes fastest.
Arguments:
- hidden: bfloat16 [512, 3584], P('grp'), may hold values from -300 to 300
- token_ids: int32 [512], P('grp'), may hold values from 0 to 131071
- serving: int32 [512], replicated, may hold values from 0 to 511, each once
- head_weight: bfloat16 [3584, 131072], P(None, ('grp', 'vocab')), may hold values from -0.3125 to 0.3125
- teacher_logits: bfloat16 [512, 4, 32768], P('grp', None, 'vocab'), may hold values from -300 to 300
Outputs:
- grad_hidden: float32 [512, 3584], P(('grp', 'vocab'))
- grad_head: bfloat16 [3584, 131072], P(None, ('grp', 'vocab'))
All inputs are finite; a program needn't handle non-finite values.
Results may differ from a plain program's by a relative error of at most 0.012.
Values may be sent and summed in bfloat16 or wider, within the bound.
A program may use at most 128 MiB of HBM per device.

v0:
```python
import jax
import jax.numpy as jnp
from jax import lax
from jax.sharding import PartitionSpec as P

smoothing_divisor = 2.0
imitation_mixing_coefficient = 0.5
objective_scaling_factor = 32.0


def body(hidden, token_ids, serving, head_weight, teacher_logits):
    rows_all, ids_all = (
        lax.all_gather(hidden, "grp", axis=0, tiled=True),
        lax.all_gather(token_ids, "grp", axis=0, tiled=True),
    )
    groups = lax.axis_size("grp")
    shards = lax.axis_size("vocab")
    arrived = lax.all_to_all(teacher_logits, "grp", split_axis=1, concat_axis=0, tiled=True)
    per_group = arrived.shape[0] // groups
    shard_cols = head_weight.shape[1]
    mentor_activations = arrived.reshape(groups * per_group, shard_cols)[serving].astype(
        jnp.float32
    )
    logits = jnp.dot(rows_all, head_weight, preferred_element_type=jnp.float32)
    local_peak = jnp.max(logits, axis=1)
    local_tpeak = jnp.max(mentor_activations, axis=1)
    student_peak, mentor_peak_activation = lax.pmax((local_peak, local_tpeak), ("grp", "vocab"))
    shifted_pupil_activations = logits - student_peak[:, None]
    mentor_shifted_activations = (
        mentor_activations - mentor_peak_activation[:, None]
    ) / smoothing_divisor
    sum_hard, mentor_component_accumulated, mentor_exponential_summed = lax.psum(
        (
            jnp.sum(jnp.exp(shifted_pupil_activations), axis=1),
            jnp.sum(jnp.exp(shifted_pupil_activations / smoothing_divisor), axis=1),
            jnp.sum(jnp.exp(mentor_shifted_activations), axis=1),
        ),
        ("grp", "vocab"),
    )
    first_col = (lax.axis_index("grp") * shards + lax.axis_index("vocab")) * shard_cols
    columns = first_col + jnp.arange(shard_cols, dtype=jnp.int32)
    labels = (ids_all[:, None] == columns[None, :]).astype(jnp.float32)
    mentor_match_component = (
        jnp.exp(shifted_pupil_activations / smoothing_divisor)
        / mentor_component_accumulated[:, None]
        - jnp.exp(mentor_shifted_activations) / mentor_exponential_summed[:, None]
    )
    ground_truth_component = jnp.exp(shifted_pupil_activations) / sum_hard[:, None] - labels
    activation_derivative = (
        objective_scaling_factor
        * (
            imitation_mixing_coefficient * smoothing_divisor * mentor_match_component
            + (1.0 - imitation_mixing_coefficient) * ground_truth_component
        )
    ).astype(jnp.bfloat16)
    grad_head = lax.dot_general(
        rows_all,
        activation_derivative,
        (((0,), (0,)), ((), ())),
        preferred_element_type=jnp.float32,
    ).astype(jnp.bfloat16)
    grad_hidden = lax.psum_scatter(
        lax.dot_general(
            activation_derivative,
            head_weight,
            (((1,), (1,)), ((), ())),
            preferred_element_type=jnp.float32,
        ),
        ("grp", "vocab"),
        scatter_dimension=0,
        tiled=True,
    )
    return (grad_hidden, grad_head)


def solution(mesh):
    placed = (P("grp", None), P("grp"), P(), P(None, ("grp", "vocab")), P("grp", None, "vocab"))
    return jax.shard_map(
        body,
        mesh=mesh,
        in_specs=placed,
        out_specs=(P(("grp", "vocab"), None), P(None, ("grp", "vocab"))),
        check_vma=False,
    )
```

profile of v0, /device:TPU:2, one launch (start us, length us, event | category | flops | bytes accessed | tf_op | source)
XLA Modules:
  0.0 496.0 jit_solution(7717538703475757772)
XLA Ops:
  7.2 0.0 all-gather.3.cloned.1.call-start
  7.2 0.7 all-gather.3.cloned.1.call-update
  7.9 1.9 copy.10
  9.8 3.5 all-to-all-start
  13.3 0.0 all-reduce.5.cloned.1.call-start
  13.4 11.1 %all-gather = s32[4,1,128]{2,1,0:T(1,128)S(1)} all-gather(s32[1,1,128]{2,1,0:T(1,128)} %bitcast.16), channel_id=1, replica_groups=mesh['grp'=4,'vocab'=64] {'grp'}, dimensions={0}, use_global_device_ids=true | all-gather | bytes 2560 | tf_op jit(solution)/shard_map/all_gather | solution.py:14
  24.5 0.7 compare_select_fusion
  25.2 0.0 all-to-all-done
  25.2 2.0 gather_fusion
  27.2 0.2 copy.11
  27.4 0.2 reduce_max.24
  27.6 22.4 %all-gather.3.cloned.1.call-done = bf16[512,3584]{1,0:T(8,128)(2,1)} async-done(((bf16[128,3584]{1,0:T(8,128)(2,1)}), bf16[512,3584]{1,0:T(8,128)(2,1)}) %all-gather.3.cloned.1.call-update) | async-done | bytes 3670032 | tf_op jit(solution)/shard_map/all_gather | solution.py:13
  50.0 5.3 %fusion.4 = (f32[512]{0:T(512)S(1)}, f32[512,512]{0,1:T(8,128)S(1)}) fusion(bf16[512,3584]{1,0:T(8,128)(2,1)} %all-gather.3.cloned.1.call-done, bf16[3584,512]{1,0:T(8,128)(2,1)} %param.8), kind=kOutput, calls=%fused_computation.14 | convolution fusion | flops 1879309824 | bytes 8390656 | tf_op jit(solution)/shard_map/dot_general | solution.py:24
  55.3 76.9 %all-reduce.2 = (f32[512]{0:T(512)S(1)}, f32[512]{0:T(512)S(1)}) all-reduce(f32[512]{0:T(512)S(1)} %get-tuple-element.13, bf16[512]{0:T(512)(128)(2,1)S(1)} %reduce_max.24), channel_id=1, replica_groups=mesh['grp'=4,'vocab'=64] {'grp','vocab'}, use_global_device_ids=true, to_apply=%region_1.0 | all-reduce | flops 1024 | bytes 7168 | tf_op jit(solution)/shard_map/pmax | solution.py:27
  132.1 0.5 fusion.2
  132.6 74.3 %all-reduce.1 = (f32[512]{0:T(512)S(1)}, f32[512]{0:T(512)S(1)}, f32[512]{0:T(512)S(1)}) all-reduce(f32[512]{0:T(512)S(1)} %get-tuple-element.7, f32[512]{0:T(512)S(1)} %get-tuple-element.15, f32[512]{0:T(512)S(1)} %get-tuple-element.6), channel_id=1, replica_groups=mesh['grp'=4,'vocab'=64] {'grp','vocab'}, use_global_device_ids=true, to_apply=%region_9.0 | all-reduce | flops 1536 | bytes 12288 | tf_op jit(solution)/shard_map/psum | solution.py:32
  206.9 7.7 %fusion.3 = f32[512,3584]{1,0:T(8,128)} fusion(bf16[3584,512]{1,0:T(8,128)(2,1)} %param.8, bf16[512,512]{0,1:T(8,128)(2,1)S(1)} %copy.11, f32[512,512]{0,1:T(8,128)S(1)} %get-tuple-element.14, s32[512]{0:T(512)S(1)} %bitcast.14, f32[512]{0:T(512)S(1)} %get-tuple-element.8, f32[512]{0:T(512)S(1)} %get-tuple-element.9, f32[512]{0:T(512)S(1)} %get-tuple-element.12, ...), kind=kOutput, calls=%fused_computation.13 | convolution fusion | flops 1883242496 | bytes 12597248 | tf_op jit(solution)/shard_map/dot_general | solution.py:63
  214.7 0.0 all-reduce.5.cloned.1.call-update
  214.7 6.5 %fusion = bf16[3584,512]{0,1:T(8,128)(2,1)} fusion(bf16[512,3584]{1,0:T(8,128)(2,1)} %all-gather.3.cloned.1.call-done, bf16[512,512]{0,1:T(8,128)(2,1)S(1)} %copy.11, f32[512,512]{0,1:T(8,128)S(1)} %get-tuple-element.14, s32[512]{0:T(512)S(1)} %bitcast.15, f32[512]{0:T(512)S(1)} %get-tuple-element.8, f32[512]{0:T(512)S(1)} %get-tuple-element.9, ...), kind=kOutput, calls=%fused_computation.2 | convolution fusion | flops 1885077504 | bytes 8927232 | tf_op jit(solution)/shard_map/dot_general | solution.py:56
  221.2 5.9 %copy.12 = bf16[3584,512]{1,0:T(8,128)(2,1)} copy(bf16[3584,512]{0,1:T(8,128)(2,1)} %fusion) | data formatting | bytes 7340032
  227.2 260.5 %all-reduce.5.cloned.1.call-done = f32[512,3584]{1,0:T(8,128)} async-done(((f32[512,3584]{1,0:T(8,128)}), f32[512,3584]{1,0:T(8,128)}) %all-reduce.5.cloned.1.call-update) | async-done | bytes 7340048
  487.7 1.5 constant_dynamic-slice_fusion
  (2 shorter events, 0.0 us)
Async XLA Ops:
  7.2 42.8 %all-gather.3.cloned.1.call-start = ((), (), s32[]{:S(2)}) async-start(), calls=%async_computation.1 | async-start | bytes 4587520 | tf_op jit(solution)/shard_map/all_gather | solution.py:13
  9.8 15.4 %all-to-all-start = ((bf16[128,4,512]{2,0,1:T(8,128)(2,1)}), bf16[128,4,512]{2,0,1:T(8,128)(2,1)S(1)}, u32[]{:S(2)}, u32[]{:S(2)}) async-start(bf16[128,4,512]{2,0,1:T(8,128)(2,1)} %copy.10), calls=%async_computation | async-start | bytes 1048576 | tf_op jit(solution)/shard_map/all_to_all | solution.py:18
  13.3 474.4 %all-reduce.5.cloned.1.call-start = ((), (), s32[]{:S(2)}) async-start(), calls=%async_computation.2 | async-start | bytes 14680064
Sparse Core Ops, SparseCore 0:
  9.8 40.1 all-gather.2
  214.8 272.7 all-reduce.4
where the time goes:
time: 497 us; the launch traced here: 496 us
  waiting for transfers between devices  284 us (57%)
  blocking collectives  162 us (33%)
  matrix products  19.5 us (4%)
  between operations  14.1 us (3%)
  local copies, waits for them, and re-layouts  11.5 us (2%)
    unnamed x3, waiting for transfers between devices  261 us
    pmax x1, blocking collectives, body(): lax.pmax((local_peak, local_tpeak), ('grp', 'vocab'))  76.9 us
    psum x1, blocking collectives, body(): lax.psum((jnp.sum(jnp.exp(shifted_pupil_activations), axis=1), jnp.sum(jn...  74.3 us
    all_gather x1, waiting for transfers between devices, body(): lax.all_gather(hidden, 'grp', axis=0, tiled=True)  22.4 us
    all_gather x1, blocking collectives, body(): lax.all_gather(token_ids, 'grp', axis=0, tiled=True)  11.1 us
  transfers between devices with their start and end apart: 3, of which 2 were waited for; matrix products, arithmetic and copies ran while one was open for 4% of the time, Pallas kernels for 0%

commit v1 on v0

v1 whole, which is shorter than its diff:
```python
import functools

import jax
import jax.numpy as jnp
from jax import lax
from jax.experimental import pallas as pl
from jax.experimental.pallas import tpu as pltpu
from jax.sharding import PartitionSpec as P

MESH = pl.DeviceIdType.MESH
F32 = jnp.float32
BF16 = jnp.bfloat16
I32 = jnp.int32

DS = 3584
COLS = 512
GRPS = 4
ROWS = 512
GROWS = 128
NX, NY, NZ = 4, 4, 8

Y0 = 384
Y1 = 256
ZW = 128
YB1 = NY * Y0
ZB = YB1 + NY * Y1

NCH = 4
CW = DS // NCH

HCH = 7
HW = DS // HCH


def device(x, y, z, c):
    return (lax.div(x, 2) * 2 + c, (z * 2 + lax.rem(x, 2)) * 4 + y)


def merge(blocks):
    ms = functools.reduce(jnp.maximum, [b[0:1] for b in blocks])
    mt = functools.reduce(jnp.maximum, [b[1:2] for b in blocks])
    hard = soft = teach = 0.0
    for b in blocks:
        d = jnp.exp((b[0:1] - ms) * 0.5)
        hard = hard + b[2:3] * (d * d)
        soft = soft + b[3:4] * d
        teach = teach + b[4:5] * jnp.exp((b[1:2] - mt) * 0.5)
    return ms, mt, hard, soft, teach


def kernel(
    hid, ids, srv, w_hbm, t_hbm, gh_out, ghead_out,
    h_all, w, wt, ht, tv, tst, tall, ids_all, pt, perm, lg, et, stc, st, st_c, st_x, st_y, st_z, fin, fint,
    g, gp, own, dsend, drecv, s1, r1, acc, s2, r2, s3, r3, gheadv,
    ssem, rsem, lsem,
):
    gi = lax.axis_index("grp")
    vi = lax.axis_index("vocab")
    c = lax.rem(gi, 2)
    xh = lax.div(gi, 2)
    y = lax.rem(vi, 4)
    xl = lax.rem(lax.div(vi, 4), 2)
    z = lax.div(vi, 8)
    x = 2 * xh + xl
    other = device(x, y, z, 1 - c)
    partner = device(3 - x, y, z, c)
    xs = [device(lax.rem(x + k, NX), y, z, c) for k in range(1, NX)]
    ys = [device(x, lax.rem(y + k, NY), z, c) for k in range(1, NY)]
    zs = [device(x, y, lax.rem(z + k, NZ), c) for k in range(1, NZ)]
    far = device(lax.rem(x + 2, NX), y, z, 1 - c)

    bar = pltpu.get_barrier_semaphore()
    peers = [other, *xs, *ys, *zs, far]
    for p in peers:
        pl.semaphore_signal(bar, inc=1, device_id=p, device_id_type=MESH)

    count = [0]
    started = []

    def send(src, dst, to):
        k = count[0]
        count[0] += 1
        cp = pltpu.make_async_remote_copy(
            src_ref=src, dst_ref=dst, send_sem=ssem.at[k], recv_sem=rsem.at[k], device_id=to, device_id_type=MESH
        )
        cp.start()
        started.append(cp)
        return cp

    load_t = pltpu.make_async_copy(t_hbm, tv, lsem.at[0])
    load_t.start()
    load_h = pltpu.make_async_copy(hid, h_all.at[gi], lsem.at[1])
    load_h.start()
    load_w = pltpu.make_async_copy(w_hbm, w, lsem.at[2])
    load_w.start()

    pt[...] = (lax.broadcasted_iota(I32, (ROWS, ROWS), 0) == srv[...]).astype(BF16)
    ids_all[gi] = ids[...]
    load_t.wait()
    for q in range(GRPS):
        tst[q] = tv[:, q, :]

    pl.semaphore_wait(bar, len(peers))

    def zcols(k):
        return pl.ds(pl.multiple_of(ZB + k * ZW, ZW), ZW)

    def ycols(j, k):
        base, width = ((0, Y0), (YB1, Y1))[j]
        return pl.ds(pl.multiple_of(base + k * width, 128), width)

    cross_z = send(hid.at[:, zcols(z)], h_all.at[gi, :, zcols(z)], partner)
    cross_y = [send(hid.at[:, ycols(j, y)], h_all.at[gi, :, ycols(j, y)], partner) for j in range(2)]
    pair = send(hid, h_all.at[gi], other)
    teach, idc = [], []
    for k in range(1, GRPS):
        q = lax.rem(gi + k, GRPS)
        to = (q, vi)
        idc.append(send(ids_all.at[gi], ids_all.at[gi], to))
        teach.append(send(tst.at[q], tall.at[gi], to))
    tall[gi] = tst[gi]

    gg = 2 * (1 - xh) + c
    cross_z.wait_recv()
    fwd_z = [send(h_all.at[gg, :, zcols(z)], h_all.at[gg, :, zcols(z)], p) for p in zs]
    fwd_y = []
    for j in range(2):
        cross_y[j].wait_recv()
        fwd_y.append([send(h_all.at[gg, :, ycols(j, y)], h_all.at[gg, :, ycols(j, y)], p) for p in ys])

    load_w.wait()
    load_h.wait()
    pair.wait_recv()

    def logits(half):
        row = pl.multiple_of(half * 256, 256)
        for j in range(2):
            a = h_all[2 * half + j]
            lg[pl.ds(pl.multiple_of(row + j * 128, 128), 128), :] = jnp.dot(a, w[...], preferred_element_type=F32)

    logits(xh)

    def turn_rows(half):
        for j in range(2):
            gr = 2 * half + j

            def step(i, _):
                s = pl.ds(pl.multiple_of(i * HW, HW), HW)
                ht[s, pl.ds(pl.multiple_of(gr * GROWS, GROWS), GROWS)] = h_all[gr, :, s].T
                return 0

            lax.fori_loop(0, HCH, step, 0)

    def student_stats(half):
        def step(j, _):
            r = pl.ds(pl.multiple_of(half * 256 + j * 128, 128), 128)
            l = lg[r, :]
            m = jnp.max(l, axis=1, keepdims=True)
            e = jnp.exp((l - m) * 0.5)
            lg[r, :] = e
            lane = lax.broadcasted_iota(I32, (128, 128), 1)
            hard = jnp.sum(e * e, axis=1, keepdims=True)
            soft = jnp.sum(e, axis=1, keepdims=True)
            stc[r, :] = jnp.where(lane == 0, m, jnp.where(lane == 2, hard, jnp.where(lane == 3, soft, stc[r, :])))
            return 0

        lax.fori_loop(0, 2, step, 0)

    def share(refs):
        return [send(h_all.at[gg, :, s], h_all.at[gg, :, s], other) for s in refs]

    for cp in fwd_z:
        cp.wait_recv()
    shared = share([pl.ds(ZB, NZ * ZW)])
    for cp in fwd_y[0]:
        cp.wait_recv()
    shared += share([pl.ds(0, YB1)])

    for cp in teach:
        cp.wait_recv()
    al = lax.dot_general(
        pt[...], tall[...].reshape(ROWS, COLS), (((0,), (0,)), ((), ())), preferred_element_type=F32
    )
    et[...] = al

    def teacher_stats(j, _):
        r = pl.ds(pl.multiple_of(j * 128, 128), 128)
        a = et[r, :]
        m = jnp.max(a, axis=1, keepdims=True)
        e = jnp.exp((a - m) * 0.5)
        et[r, :] = e
        lane = lax.broadcasted_iota(I32, (128, 128), 1)
        stc[r, :] = jnp.where(lane == 1, m, jnp.where(lane == 4, jnp.sum(e, axis=1, keepdims=True), 0.0))
        return 0

    lax.fori_loop(0, 4, teacher_stats, 0)

    for cp in fwd_y[1]:
        cp.wait_recv()
    shared += share([pl.ds(YB1, NY * Y1)])
    student_stats(xh)

    for cp in shared:
        cp.wait_recv()
    logits(1 - xh)
    student_stats(1 - xh)

    def put(ref, stats):
        for k, s in enumerate(stats):
            ref[k : k + 1, :] = s

    for j in range(4):
        st[0, :, j * 128 : (j + 1) * 128] = stc[j * 128 : (j + 1) * 128, :].T[0:8, :]
    cp = send(st.at[0], st_c, other)
    turn_rows(xh)
    cp.wait_recv()
    put(st.at[1], merge([st[0], st_c[...]]))
    cps = [send(st.at[1], st_x.at[k], p) for k, p in enumerate(xs)]
    turn_rows(1 - xh)
    for cp in cps:
        cp.wait_recv()
    put(st.at[2], merge([st[1], *[st_x[k] for k in range(NX - 1)]]))
    cps = [send(st.at[2], st_y.at[k], p) for k, p in enumerate(ys)]

    def turn_w(i, _):
        s = pl.ds(pl.multiple_of(i * HW, HW), HW)
        wt[:, s] = w[s, :].T
        return 0

    lax.fori_loop(0, HCH, turn_w, 0)
    for cp in cps:
        cp.wait_recv()
    put(st.at[3], merge([st[2], *[st_y[k] for k in range(NY - 1)]]))
    cps = [send(st.at[3], st_z.at[k], p) for k, p in enumerate(zs)]

    i = lax.broadcasted_iota(I32, (ROWS, 1), 0)
    i_c, i_x, i_y = lax.div(i, 256), lax.rem(lax.div(i, 64), 4), lax.rem(lax.div(i, 16), 4)
    i_z, i_b = lax.rem(lax.div(i, 2), 8), lax.rem(i, 2)
    r = (2 * lax.div(i_x, 2) + i_c) * 128 + i_z * 16 + lax.rem(i_x, 2) * 8 + i_y * 2 + i_b
    perm[...] = (lax.broadcasted_iota(I32, (ROWS, ROWS), 1) == r).astype(BF16)
    for cp in idc:
        cp.wait_recv()

    for cp in cps:
        cp.wait_recv()
    ms, mt, hard, soft, teach_sum = merge([st[3], *[st_z[k] for k in range(NZ - 1)]])
    d = jnp.exp((st[0, 0:1, :] - ms) * 0.5)
    fin[...] = jnp.zeros_like(fin)
    fin[0:1, :] = 32.0 * d / soft
    fin[1:2, :] = 32.0 * jnp.exp((st[0, 1:2, :] - mt) * 0.5) / teach_sum
    fin[2:3, :] = 16.0 * d * d / hard
    for j in range(4):
        fin[3:4, j * 128 : (j + 1) * 128] = ids_all[j].astype(F32)
    for j in range(4):
        fint[j * 128 : (j + 1) * 128, :] = fin[:, j * 128 : (j + 1) * 128].T

    first = (gi * (NX // 2 * NY * NZ) + vi) * COLS

    def grad(j, _):
        r = pl.ds(pl.multiple_of(j * 128, 128), 128)
        f = fint[r, :]
        e = lg[r, :]
        col = lax.broadcasted_iota(I32, (128, COLS), 1) + first
        hit = jnp.where(f[:, 3:4].astype(I32) == col, 16.0, 0.0)
        g[r, :] = (e * f[:, 0:1] - et[r, :] * f[:, 1:2] + (e * e * f[:, 2:3] - hit)).astype(BF16)
        return 0

    lax.fori_loop(0, 4, grad, 0)
    gp[...] = jnp.dot(perm[...], g[...], preferred_element_type=F32).astype(BF16)

    pairs, ones, twos = [], [], []

    def first_stage(ch):
        pairs[ch].wait_recv()

        def step(k, _):
            s1[ch, k] = (own[ch, k] + drecv[ch, k].astype(F32)).astype(BF16)
            return 0

        lax.fori_loop(0, NX, step, 0)
        if ch % 2 == 0:
            ones.append([send(s1.at[ch, lax.rem(x + k, NX)], r1.at[ch, k - 1], p) for k, p in enumerate(xs, 1)])
        else:
            ones.append([send(s1.at[ch, :, lax.rem(y + k, NY)], r1.at[ch, k - 1], p) for k, p in enumerate(ys, 1)])

    def half_rows(k):
        return gp[pl.ds(pl.multiple_of(k * 256, 256), 256), :]

    for ch in range(NCH):
        s = slice(ch * CW, (ch + 1) * CW)
        dsend[ch] = (
            jnp.dot(half_rows(1 - c), wt[:, s], preferred_element_type=F32).astype(BF16).reshape(NX, NY, 16, CW)
        )
        pairs.append(send(dsend.at[ch], drecv.at[ch], other))
        own[ch] = jnp.dot(half_rows(c), wt[:, s], preferred_element_type=F32).reshape(NX, NY, 16, CW)
        if ch:
            first_stage(ch - 1)
    first_stage(NCH - 1)

    stores = []

    def head(k):
        s = pl.ds(k * HW, HW)
        gheadv[s, :] = jnp.dot(ht[s, :], g[...], preferred_element_type=F32).astype(BF16)
        cp = pltpu.make_async_copy(gheadv.at[s], ghead_out.at[s], lsem.at[3 + k])
        cp.start()
        stores.append(cp)

    heads = list(range(HCH))

    def second_stage(ch):
        for cp in ones[ch]:
            cp.wait_recv()
        for j in range(4):
            place = (ch, x, j) if ch % 2 == 0 else (ch, j, y)
            t = own[place] + drecv[place].astype(F32)
            for k in range(3):
                t = t + r1[ch, k, j].astype(F32)
            acc[ch, j] = t
            s2[ch, j] = t.astype(BF16)
        n, me, to = (NY, y, ys) if ch % 2 == 0 else (NX, x, xs)
        twos.append([send(s2.at[ch, lax.rem(me + k, n)], r2.at[ch, k - 1], p) for k, p in enumerate(to, 1)])

    for ch in range(NCH):
        for _ in range(2):
            if heads:
                head(heads.pop(0))
        second_stage(ch)
    while heads:
        head(heads.pop(0))

    for ch in range(NCH):
        for cp in twos[ch]:
            cp.wait_recv()
        t = acc[ch, y if ch % 2 == 0 else x]
        for k in range(3):
            t = t + r2[ch, k].astype(F32)
        for j in range(NZ):
            s3[j, :, ch * CW : (ch + 1) * CW] = t[2 * j : 2 * j + 2, :]
    threes = [send(s3.at[lax.rem(z + k, NZ)], r3.at[k - 1], p) for k, p in enumerate(zs, 1)]
    for cp in threes:
        cp.wait_recv()
    t = s3[z]
    for k in range(NZ - 1):
        t = t + r3[k]
    gh_out[...] = t

    for cp in started:
        cp.wait_send()
    for cp in stores:
        cp.wait()


N_SEMS = 96


def body(hidden, token_ids, serving, head_weight, teacher_logits):
    vm = pltpu.VMEM
    return pl.pallas_call(
        kernel,
        out_shape=(
            jax.ShapeDtypeStruct((2, DS), F32),
            jax.ShapeDtypeStruct((DS, COLS), BF16),
        ),
        in_specs=[
            pl.BlockSpec(memory_space=pl.ANY),
            pl.BlockSpec(memory_space=vm),
            pl.BlockSpec(memory_space=vm),
            pl.BlockSpec(memory_space=pl.ANY),
            pl.BlockSpec(memory_space=pl.ANY),
        ],
        out_specs=(pl.BlockSpec(memory_space=vm), pl.BlockSpec(memory_space=pl.ANY)),
        scratch_shapes=[
            vm((GRPS, GROWS, DS), BF16),
            vm((DS, COLS), BF16),
            vm((COLS, DS), BF16),
            vm((DS, ROWS), BF16),
            vm((GROWS, GRPS, COLS), BF16),
            vm((GRPS, GROWS, COLS), BF16),
            vm((GRPS, GROWS, COLS), BF16),
            vm((GRPS, 1, GROWS), I32),
            vm((ROWS, ROWS), BF16),
            vm((ROWS, ROWS), BF16),
            vm((ROWS, COLS), F32),
            vm((ROWS, COLS), F32),
            vm((ROWS, 128), F32),
            vm((4, 8, ROWS), F32),
            vm((8, ROWS), F32),
            vm((NX - 1, 8, ROWS), F32),
            vm((NY - 1, 8, ROWS), F32),
            vm((NZ - 1, 8, ROWS), F32),
            vm((128, ROWS), F32),
            vm((ROWS, 128), F32),
            vm((ROWS, COLS), BF16),
            vm((ROWS, COLS), BF16),
            vm((NCH, NX, NY, 16, CW), F32),
            vm((NCH, NX, NY, 16, CW), BF16),
            vm((NCH, NX, NY, 16, CW), BF16),
            vm((NCH, NX, NY, 16, CW), BF16),
            vm((NCH, 3, 4, 16, CW), BF16),
            vm((NCH, 4, 16, CW), F32),
            vm((NCH, 4, 16, CW), BF16),
            vm((NCH, 3, 16, CW), BF16),
            vm((NZ, 2, DS), F32),
            vm((NZ - 1, 2, DS), F32),
            vm((DS, COLS), BF16),
            pltpu.SemaphoreType.DMA((N_SEMS,)),
            pltpu.SemaphoreType.DMA((N_SEMS,)),
            pltpu.SemaphoreType.DMA((3 + HCH,)),
        ],
        compiler_params=pltpu.CompilerParams(
            collective_id=0, has_side_effects=True, vmem_limit_bytes=60 * 1024 * 1024
        ),
        name="distill_backward",
    )(hidden, token_ids.reshape(1, GROWS), serving.reshape(1, ROWS), head_weight, teacher_logits)


def solution(mesh):
    placed = (P("grp", None), P("grp"), P(), P(None, ("grp", "vocab")), P("grp", None, "vocab"))
    return jax.shard_map(
        body,
        mesh=mesh,
        in_specs=placed,
        out_specs=(P(("grp", "vocab"), None), P(None, ("grp", "vocab"))),
        check_vma=False,
    )
```

time: 497 us -> 84 us (0.17)
  waiting for transfers between devices: 284 us -> 0 us
  blocking collectives: 162 us -> 0 us
  Pallas kernels: 0 us -> 77.3 us
  matrix products: 19.5 us -> 0 us
  between operations: 14.1 us -> 0.64 us
  local copies, waits for them, and re-layouts: 11.5 us -> 5.47 us
    unnamed x3 -> x0, waiting for transfers between devices: 261 us -> none
    pallas_call x0 -> x1, Pallas kernels: none -> 77.3 us  [body(): pl.pallas_call(kernel, out_shape=(jax.ShapeDtypeStruct((2, DS), F32), jax...]
    pmax x1 -> x0, blocking collectives: 76.9 us -> none  [body(): lax.pmax((local_peak, local_tpeak), ('grp', 'vocab'))]
    psum x1 -> x0, blocking collectives: 74.3 us -> none  [body(): lax.psum((jnp.sum(jnp.exp(shifted_pupil_activations), axis=1), jnp.sum(jn...]
    all_gather x1 -> x0, waiting for transfers between devices: 22.4 us -> none  [body(): lax.all_gather(hidden, 'grp', axis=0, tiled=True)]
    dot_general x3 -> x0, matrix products: 19.5 us -> none  [the longest x1 7.74 us: body(): lax.dot_general(activation_derivative, head_weight, (((1,), (1,)), ((), (...]
    all_gather x1 -> x0, blocking collectives: 11.1 us -> none  [body(): lax.all_gather(token_ids, 'grp', axis=0, tiled=True)]
  transfers between devices with their start and end apart: 3 -> 0, of which waited for: 2 -> 0; matrix products, arithmetic and copies ran while one was open for 4% -> 0% of each run, Pallas kernels for 0% -> 0%
where the time goes in v1:
time: 84 us; the launch traced here: 83.4 us
  Pallas kernels  77.3 us (92%)
  local copies, waits for them, and re-layouts  5.47 us (7%)
    pallas_call x1, Pallas kernels, body(): pl.pallas_call(kernel, out_shape=(jax.ShapeDtypeStruct((2, DS), F32), jax...  77.3 us
    unnamed x2, local copies, waits for them, and re-layouts  5.47 us

profile of v1, /device:TPU:2, one launch (start us, length us, event | category | flops | bytes accessed | tf_op | source)
XLA Modules:
  0.0 83.4 jit_solution(9571978827581968486)
XLA Ops:
  0.6 77.3 %distill_backward.1 = (f32[2,3584]{1,0:T(2,128)}, bf16[3584,512]{1,0:T(8,128)(2,1)}) custom-call(bf16[128,3584]{1,0:T(8,128)(2,1)} %hid.1, s32[1,128]{1,0:T(1,128)} %bitcast.3, s32[1,512]{1,0:T(1,128)} %bitcast.2, bf16[3584,512]{1,0:T(8,128)(2,1)} %w_hbm.1, bf16[128,4,512]{2,1,0:T(4,128)(2,1)} %t_hbm.1), custom_call_target="tpu_custom_call" | custom-call | tf_op jit(solution)/shard_map/distill_backward/pallas_call | solution.py:359
  78.0 1.4 %copy.9 = f32[2,3584]{1,0:T(2,128)} copy(f32[2,3584]{1,0:T(2,128)} %get-tuple-element.4) | data formatting | bytes 57344
  79.3 4.1 %copy.10 = bf16[3584,512]{1,0:T(8,128)(2,1)} copy(bf16[3584,512]{1,0:T(8,128)(2,1)} %get-tuple-element.5) | data formatting | bytes 7340032

commit v2 on v1

--- a/solution.py
+++ b/solution.py
@@ -38,20 +38,20 @@
 
 def merge(blocks):
     ms = functools.reduce(jnp.maximum, [b[0:1] for b in blocks])
-    mt = functools.reduce(jnp.maximum, [b[1:2] for b in blocks])
+    mt = functools.reduce(jnp.maximum, [b[3:4] for b in blocks])
     hard = soft = teach = 0.0
     for b in blocks:
         d = jnp.exp((b[0:1] - ms) * 0.5)
-        hard = hard + b[2:3] * (d * d)
-        soft = soft + b[3:4] * d
-        teach = teach + b[4:5] * jnp.exp((b[1:2] - mt) * 0.5)
-    return ms, mt, hard, soft, teach
+        hard = hard + b[1:2] * (d * d)
+        soft = soft + b[2:3] * d
+        teach = teach + jnp.exp(b[3:4] - mt)
+    return ms, hard, soft, mt + jnp.log(teach)
 
 
 def kernel(
-    hid, ids, srv, w_hbm, t_hbm, gh_out, ghead_out,
-    h_all, w, wt, ht, tv, tst, tall, ids_all, pt, perm, lg, et, stc, st, st_c, st_x, st_y, st_z, fin, fint,
-    g, gp, own, dsend, drecv, s1, r1, acc, s2, r2, s3, r3, gheadv,
+    hid, ids_hbm, srv_hbm, w_hbm, t_hbm, gh_out, ghead_out,
+    ids, srv, h_all, w, wt, ht, tv, tst, tall, ids_all, pt, perm, lg, et, stc, st, st_c, st_x, st_y, st_z, fin, fint,
+    g, gp, own, dsend, drecv, s1, r1, acc, s2, r2, acc3, s3f, s3, r3,
     ssem, rsem, lsem,
 ):
     gi = lax.axis_index("grp")
@@ -87,6 +87,9 @@
         started.append(cp)
         return cp
 
+    load_s = [pltpu.make_async_copy(ids_hbm, ids, lsem.at[3]), pltpu.make_async_copy(srv_hbm, srv, lsem.at[4])]
+    for cp in load_s:
+        cp.start()
     load_t = pltpu.make_async_copy(t_hbm, tv, lsem.at[0])
     load_t.start()
     load_h = pltpu.make_async_copy(hid, h_all.at[gi], lsem.at[1])
@@ -94,31 +97,33 @@
     load_w = pltpu.make_async_copy(w_hbm, w, lsem.at[2])
     load_w.start()
 
+    for cp in load_s:
+        cp.wait()
     pt[...] = (lax.broadcasted_iota(I32, (ROWS, ROWS), 0) == srv[...]).astype(BF16)
     ids_all[gi] = ids[...]
+    pl.semaphore_wait(bar, len(peers))
+
+    def zcols(k):
+        return pl.ds(pl.multiple_of(ZB + k * ZW, ZW), ZW)
+
+    def ycols(j, k):
+        base, width = ((0, Y0), (YB1, Y1))[j]
+        return pl.ds(pl.multiple_of(base + k * width, 128), width)
+
+    cross_z = send(hid.at[:, zcols(z)], h_all.at[gi, :, zcols(z)], partner)
+    cross_y = [send(hid.at[:, ycols(j, y)], h_all.at[gi, :, ycols(j, y)], partner) for j in range(2)]
+    pair = send(hid, h_all.at[gi], other)
+    idc = [send(ids_all.at[gi], ids_all.at[gi], (lax.rem(gi + k, GRPS), vi)) for k in range(1, GRPS)]
+
     load_t.wait()
     for q in range(GRPS):
         tst[q] = tv[:, q, :]
-
-    pl.semaphore_wait(bar, len(peers))
-
-    def zcols(k):
-        return pl.ds(pl.multiple_of(ZB + k * ZW, ZW), ZW)
-
-    def ycols(j, k):
-        base, width = ((0, Y0), (YB1, Y1))[j]
-        return pl.ds(pl.multiple_of(base + k * width, 128), width)
-
-    cross_z = send(hid.at[:, zcols(z)], h_all.at[gi, :, zcols(z)], partner)
-    cross_y = [send(hid.at[:, ycols(j, y)], h_all.at[gi, :, ycols(j, y)], partner) for j in range(2)]
-    pair = send(hid, h_all.at[gi], other)
-    teach, idc = [], []
-    for k in range(1, GRPS):
-        q = lax.rem(gi + k, GRPS)
-        to = (q, vi)
-        idc.append(send(ids_all.at[gi], ids_all.at[gi], to))
-        teach.append(send(tst.at[q], tall.at[gi], to))
-    tall[gi] = tst[gi]
+    t_all = tst[...].astype(F32)
+    tm = jnp.max(jnp.max(t_all, axis=0), axis=1, keepdims=True)
+    tsum = jnp.sum(jnp.sum(jnp.exp((t_all - tm[None]) * 0.5), axis=0), axis=1, keepdims=True)
+    lse = jnp.broadcast_to(tm * 0.5 + jnp.log(tsum), (GROWS, 128))
+    st[0, 3:4, :] = jnp.full((1, ROWS), -1e30, F32)
+    st[0, 3:4, pl.ds(pl.multiple_of(gi * GROWS, GROWS), GROWS)] = lse.T[0:1, :]
 
     gg = 2 * (1 - xh) + c
     cross_z.wait_recv()
@@ -127,6 +132,12 @@
     for j in range(2):
         cross_y[j].wait_recv()
         fwd_y.append([send(h_all.at[gg, :, ycols(j, y)], h_all.at[gg, :, ycols(j, y)], p) for p in ys])
+
+    teach = []
+    for k in range(1, GRPS):
+        q = lax.rem(gi + k, GRPS)
+        teach.append(send(tst.at[q], tall.at[gi], (q, vi)))
+    tall[gi] = tst[gi]
 
     load_w.wait()
     load_h.wait()
@@ -161,7 +172,7 @@
             lane = lax.broadcasted_iota(I32, (128, 128), 1)
             hard = jnp.sum(e * e, axis=1, keepdims=True)
             soft = jnp.sum(e, axis=1, keepdims=True)
-            stc[r, :] = jnp.where(lane == 0, m, jnp.where(lane == 2, hard, jnp.where(lane == 3, soft, stc[r, :])))
+            stc[r, :] = jnp.where(lane == 0, m, jnp.where(lane == 1, hard, soft))
             return 0
 
         lax.fori_loop(0, 2, step, 0)
@@ -175,25 +186,6 @@
     for cp in fwd_y[0]:
         cp.wait_recv()
     shared += share([pl.ds(0, YB1)])
-
-    for cp in teach:
-        cp.wait_recv()
-    al = lax.dot_general(
-        pt[...], tall[...].reshape(ROWS, COLS), (((0,), (0,)), ((), ())), preferred_element_type=F32
-    )
-    et[...] = al
-
-    def teacher_stats(j, _):
-        r = pl.ds(pl.multiple_of(j * 128, 128), 128)
-        a = et[r, :]
-        m = jnp.max(a, axis=1, keepdims=True)
-        e = jnp.exp((a - m) * 0.5)
-        et[r, :] = e
-        lane = lax.broadcasted_iota(I32, (128, 128), 1)
-        stc[r, :] = jnp.where(lane == 1, m, jnp.where(lane == 4, jnp.sum(e, axis=1, keepdims=True), 0.0))
-        return 0
-
-    lax.fori_loop(0, 4, teacher_stats, 0)
 
     for cp in fwd_y[1]:
         cp.wait_recv()
@@ -210,7 +202,7 @@
             ref[k : k + 1, :] = s
 
     for j in range(4):
-        st[0, :, j * 128 : (j + 1) * 128] = stc[j * 128 : (j + 1) * 128, :].T[0:8, :]
+        st[0, 0:3, j * 128 : (j + 1) * 128] = stc[j * 128 : (j + 1) * 128, :].T[0:3, :]
     cp = send(st.at[0], st_c, other)
     turn_rows(xh)
     cp.wait_recv()
@@ -240,17 +232,27 @@
     perm[...] = (lax.broadcasted_iota(I32, (ROWS, ROWS), 1) == r).astype(BF16)
     for cp in idc:
         cp.wait_recv()
+    for cp in teach:
+        cp.wait_recv()
+    et[...] = lax.dot_general(
+        pt[...], tall[...].reshape(ROWS, COLS), (((0,), (0,)), ((), ())), preferred_element_type=F32
+    )
+    fin[...] = jnp.zeros_like(fin)
+    for j in range(4):
+        fin[2:3, j * 128 : (j + 1) * 128] = ids_all[j].astype(F32)
 
     for cp in cps:
         cp.wait_recv()
-    ms, mt, hard, soft, teach_sum = merge([st[3], *[st_z[k] for k in range(NZ - 1)]])
+    ms, hard, soft, lse = merge([st[3], *[st_z[k] for k in range(NZ - 1)]])
     d = jnp.exp((st[0, 0:1, :] - ms) * 0.5)
-    fin[...] = jnp.zeros_like(fin)
     fin[0:1, :] = 32.0 * d / soft
-    fin[1:2, :] = 32.0 * jnp.exp((st[0, 1:2, :] - mt) * 0.5) / teach_sum
-    fin[2:3, :] = 16.0 * d * d / hard
-    for j in range(4):
-        fin[3:4, j * 128 : (j + 1) * 128] = ids_all[j].astype(F32)
+    fin[1:2, :] = 16.0 * d * d / hard
+    for k in range(3):
+        term = lse.astype(BF16).astype(F32)
+        fin[8 + k : 9 + k, :] = term
+        lse = lse - term
+    terms = jnp.dot(fin[8:16, :].astype(BF16), pt[...], preferred_element_type=F32)
+    fin[3:4, :] = terms[0:1] + terms[1:2] + terms[2:3]
     for j in range(4):
         fint[j * 128 : (j + 1) * 128, :] = fin[:, j * 128 : (j + 1) * 128].T
 
@@ -261,8 +263,9 @@
         f = fint[r, :]
         e = lg[r, :]
         col = lax.broadcasted_iota(I32, (128, COLS), 1) + first
-        hit = jnp.where(f[:, 3:4].astype(I32) == col, 16.0, 0.0)
-        g[r, :] = (e * f[:, 0:1] - et[r, :] * f[:, 1:2] + (e * e * f[:, 2:3] - hit)).astype(BF16)
+        hit = jnp.where(f[:, 2:3].astype(I32) == col, 16.0, 0.0)
+        soft = e * f[:, 0:1] - 32.0 * jnp.exp(et[r, :] * 0.5 - f[:, 3:4])
+        g[r, :] = (soft + (e * e * f[:, 1:2] - hit)).astype(BF16)
         return 0
 
     lax.fori_loop(0, 4, grad, 0)
@@ -297,14 +300,10 @@
             first_stage(ch - 1)
     first_stage(NCH - 1)
 
-    stores = []
 
     def head(k):
         s = pl.ds(k * HW, HW)
-        gheadv[s, :] = jnp.dot(ht[s, :], g[...], preferred_element_type=F32).astype(BF16)
-        cp = pltpu.make_async_copy(gheadv.at[s], ghead_out.at[s], lsem.at[3 + k])
-        cp.start()
-        stores.append(cp)
+        ghead_out[s, :] = jnp.dot(ht[s, :], g[...], preferred_element_type=F32).astype(BF16)
 
     heads = list(range(HCH))
 
@@ -335,19 +334,33 @@
         t = acc[ch, y if ch % 2 == 0 else x]
         for k in range(3):
             t = t + r2[ch, k].astype(F32)
-        for j in range(NZ):
-            s3[j, :, ch * CW : (ch + 1) * CW] = t[2 * j : 2 * j + 2, :]
+        acc3[:, ch * CW : (ch + 1) * CW] = t
+    s3f[:, 14:16, :] = jnp.zeros((NZ, 2, 512), F32)
+    for j in range(NZ):
+        for k in range(DS // 512):
+            s3f[j, 2 * k : 2 * k + 2, :] = acc3[2 * j : 2 * j + 2, k * 512 : (k + 1) * 512]
+    s3[...] = s3f[...].astype(BF16)
     threes = [send(s3.at[lax.rem(z + k, NZ)], r3.at[k - 1], p) for k, p in enumerate(zs, 1)]
     for cp in threes:
         cp.wait_recv()
-    t = s3[z]
+    t = s3f[z]
     for k in range(NZ - 1):
-        t = t + r3[k]
-    gh_out[...] = t
+        t = t + r3[k].astype(F32)
+    for k in range(DS // 512):
+        gh_out[:, k * 512 : (k + 1) * 512] = t[2 * k : 2 * k + 2, :]
 
     for cp in started:
         cp.wait_send()
-    for cp in stores:
+
+
+def write_out(sums, head, gh_out, ghead_out, sem):
+    cps = [pltpu.make_async_copy(sums, gh_out, sem.at[HCH])]
+    for k in range(HCH):
+        s = pl.ds(k * HW, HW)
+        cps.append(pltpu.make_async_copy(head.at[s], ghead_out.at[s], sem.at[k]))
+    for cp in cps:
+        cp.start()
+    for cp in cps:
         cp.wait()
 
 
@@ -356,21 +369,17 @@
 
 def body(hidden, token_ids, serving, head_weight, teacher_logits):
     vm = pltpu.VMEM
-    return pl.pallas_call(
+    sums, head = pl.pallas_call(
         kernel,
         out_shape=(
-            jax.ShapeDtypeStruct((2, DS), F32),
-            jax.ShapeDtypeStruct((DS, COLS), BF16),
+            vm((2, DS), F32),
+            vm((DS, COLS), BF16),
         ),
-        in_specs=[
-            pl.BlockSpec(memory_space=pl.ANY),
-            pl.BlockSpec(memory_space=vm),
-            pl.BlockSpec(memory_space=vm),
-            pl.BlockSpec(memory_space=pl.ANY),
-            pl.BlockSpec(memory_space=pl.ANY),
-        ],
-        out_specs=(pl.BlockSpec(memory_space=vm), pl.BlockSpec(memory_space=pl.ANY)),
+        in_specs=[pl.BlockSpec(memory_space=pltpu.HBM)] * 5,
+        out_specs=(pl.BlockSpec(memory_space=vm), pl.BlockSpec(memory_space=vm)),
         scratch_shapes=[
+            vm((1, GROWS), I32),
+            vm((1, ROWS), I32),
             vm((GRPS, GROWS, DS), BF16),
             vm((DS, COLS), BF16),
             vm((COLS, DS), BF16),
@@ -384,11 +393,11 @@
             vm((ROWS, COLS), F32),
             vm((ROWS, COLS), F32),
             vm((ROWS, 128), F32),
-            vm((4, 8, ROWS), F32),
-            vm((8, ROWS), F32),
-            vm((NX - 1, 8, ROWS), F32),
-            vm((NY - 1, 8, ROWS), F32),
-            vm((NZ - 1, 8, ROWS), F32),
+            vm((4, 4, ROWS), F32),
+            vm((4, ROWS), F32),
+            vm((NX - 1, 4, ROWS), F32),
+            vm((NY - 1, 4, ROWS), F32),
+            vm((NZ - 1, 4, ROWS), F32),
             vm((128, ROWS), F32),
             vm((ROWS, 128), F32),
             vm((ROWS, COLS), BF16),
@@ -401,18 +410,34 @@
             vm((NCH, 4, 16, CW), F32),
             vm((NCH, 4, 16, CW), BF16),
             vm((NCH, 3, 16, CW), BF16),
-            vm((NZ, 2, DS), F32),
-            vm((NZ - 1, 2, DS), F32),
-            vm((DS, COLS), BF16),
+            vm((16, DS), F32),
+            vm((NZ, 16, 512), F32),
+            vm((NZ, 16, 512), BF16),
+            vm((NZ - 1, 16, 512), BF16),
             pltpu.SemaphoreType.DMA((N_SEMS,)),
             pltpu.SemaphoreType.DMA((N_SEMS,)),
-            pltpu.SemaphoreType.DMA((3 + HCH,)),
+            pltpu.SemaphoreType.DMA((5,)),
         ],
         compiler_params=pltpu.CompilerParams(
-            collective_id=0, has_side_effects=True, vmem_limit_bytes=60 * 1024 * 1024
+            collective_id=0, has_side_effects=True, vmem_limit_bytes=48 * 1024 * 1024
         ),
         name="distill_backward",
-    )(hidden, token_ids.reshape(1, GROWS), serving.reshape(1, ROWS), head_weight, teacher_logits)
+    )(*[
+        pltpu.with_memory_space_constraint(a, pltpu.HBM)
+        for a in (hidden, token_ids.reshape(1, GROWS), serving.reshape(1, ROWS), head_weight, teacher_logits)
+    ])
+    return pl.pallas_call(
+        write_out,
+        out_shape=(
+            jax.ShapeDtypeStruct((2, DS), F32),
+            jax.ShapeDtypeStruct((DS, COLS), BF16),
+        ),
+        in_specs=[pl.BlockSpec(memory_space=vm)] * 2,
+        out_specs=(pl.BlockSpec(memory_space=pl.ANY), pl.BlockSpec(memory_space=pl.ANY)),
+        scratch_shapes=[pltpu.SemaphoreType.DMA((1 + HCH,))],
+        compiler_params=pltpu.CompilerParams(vmem_limit_bytes=1024 * 1024),
+        name="write_out",
+    )(sums, head)
 
 
 def solution(mesh):

time: 84 us -> 70.5 us (0.84)
  Pallas kernels: 77.3 us -> 69 us
  local copies, waits for them, and re-layouts: 5.47 us -> 0 us
    pallas_call x1 -> x2, Pallas kernels: 77.3 us -> 69 us  [the longest x1 67.1 us: body(): pl.pallas_call(kernel, out_shape=(vm((2, DS), F32), vm((DS, COLS), BF16))...]
    unnamed x2 -> x0, local copies, waits for them, and re-layouts: 5.47 us -> none
where the time goes in v2:
time: 70.5 us; the launch traced here: 69.6 us
  Pallas kernels  69 us (98%)
    pallas_call x1, Pallas kernels, body(): pl.pallas_call(kernel, out_shape=(vm((2, DS), F32), vm((DS, COLS), BF16))...  67.1 us
    pallas_call x1, Pallas kernels, body(): pl.pallas_call(write_out, out_shape=(jax.ShapeDtypeStruct((2, DS), F32),...  1.91 us

profile of v2, /device:TPU:2, one launch (start us, length us, event | category | flops | bytes accessed | tf_op | source)
XLA Modules:
  0.0 69.6 jit_solution(6583693658576926630)
XLA Ops:
  0.6 67.1 %distill_backward.1 = (f32[2,3584]{1,0:T(2,128)S(1)}, bf16[3584,512]{1,0:T(8,128)(2,1)S(1)}) custom-call(bf16[128,3584]{1,0:T(8,128)(2,1)} %hid.1, s32[1,128]{1,0:T(1,128)} %bitcast.3, s32[1,512]{1,0:T(1,128)} %bitcast.2, bf16[3584,512]{1,0:T(8,128)(2,1)} %w_hbm.1, bf16[128,4,512]{2,1,0:T(4,128)(2,1)} %t_hbm.1), custom_call_target="tpu_custom_call" | custom-call | tf_op jit(solution)/shard_map/distill_backward/pallas_call | solution.py:372
  67.7 1.9 %write_out.1 = (f32[2,3584]{1,0:T(2,128)}, bf16[3584,512]{1,0:T(8,128)(2,1)}) custom-call(f32[2,3584]{1,0:T(2,128)S(1)} %get-tuple-element.4.sums, bf16[3584,512]{1,0:T(8,128)(2,1)S(1)} %get-tuple-element.5.head), custom_call_target="tpu_custom_call" | custom-call | tf_op jit(solution)/shard_map/write_out/pallas_call | solution.py:429

commit v3 on v0

v3 whole, which is shorter than its diff:
```python
import functools

import jax
import jax.numpy as jnp
from jax import lax
from jax.experimental import pallas as pl
from jax.experimental.pallas import tpu as pltpu
from jax.sharding import PartitionSpec as P

MESH = pl.DeviceIdType.MESH
F32 = jnp.float32
BF16 = jnp.bfloat16
I32 = jnp.int32

DS = 3584
COLS = 512
GRPS = 4
ROWS = 512
GROWS = 128
NX, NY, NZ = 4, 4, 8

HROWS = GROWS // 2
HALF = ROWS // 2

YW = 640
ZW = 128
ZB = NY * YW

CW = DS // 2

HCH = 7
HW = DS // HCH


def device(x, y, z, c):
    return (lax.div(x, 2) * 2 + c, (z * 2 + lax.rem(x, 2)) * 4 + y)


def merge(blocks):
    ms = functools.reduce(jnp.maximum, [b[0:1] for b in blocks])
    hard = soft = 0.0
    for b in blocks:
        d = jnp.exp((b[0:1] - ms) * 0.5)
        hard = hard + b[1:2] * (d * d)
        soft = soft + b[2:3] * d
    if blocks[0].shape[0] == 4:
        return ms, hard, soft
    mt = functools.reduce(jnp.maximum, [b[3:5] for b in blocks])
    teach = 0.0
    for b in blocks:
        teach = teach + jnp.exp(b[3:5] - mt)
    return ms, hard, soft, mt + jnp.log(teach)


def put(ref, stats):
    k = 0
    for s in stats:
        ref[k : k + s.shape[0], :] = s
        k += s.shape[0]


def kernel(
    hid, ids_hbm, srv_hbm, w_hbm, t_hbm, gh_out, ghead_out,
    ids, srv, h_all, w, wt, ht, tv, tst, tall, ids_all, pt, perm, lg, al, stc,
    sta, sta_c, sta_x, sta_y, sta_z, stb, stb_c, stb_x, stb_y, stb_z,
    fin, fint, rowf, rowt, g, gp, own, dsend, drecv, s1, r1, s1b, r1b, acc, s2, r2, acc3, s3f, s3, r3,
    ssem, rsem, lsem,
):
    gi = lax.axis_index("grp")
    vi = lax.axis_index("vocab")
    c = lax.rem(gi, 2)
    xh = lax.div(gi, 2)
    y = lax.rem(vi, 4)
    xl = lax.rem(lax.div(vi, 4), 2)
    z = lax.div(vi, 8)
    x = 2 * xh + xl
    other = device(x, y, z, 1 - c)
    partner = device(3 - x, y, z, c)
    xs = [device(lax.rem(x + k, NX), y, z, c) for k in range(1, NX)]
    ys = [device(x, lax.rem(y + k, NY), z, c) for k in range(1, NY)]
    zs = [device(x, y, lax.rem(z + k, NZ), c) for k in range(1, NZ)]
    far = device(lax.rem(x + 2, NX), y, z, 1 - c)

    bar = pltpu.get_barrier_semaphore()
    peers = [other, *xs, *ys, *zs, far]
    for p in peers:
        pl.semaphore_signal(bar, inc=1, device_id=p, device_id_type=MESH)

    count = [0]
    started = []

    def send(src, dst, to):
        k = count[0]
        count[0] += 1
        cp = pltpu.make_async_remote_copy(
            src_ref=src, dst_ref=dst, send_sem=ssem.at[k], recv_sem=rsem.at[k], device_id=to, device_id_type=MESH
        )
        cp.start()
        started.append(cp)
        return cp

    def load(src, dst, k):
        cp = pltpu.make_async_copy(src, dst, lsem.at[k])
        cp.start()
        return cp

    def await_all(cps):
        for cp in cps:
            cp.wait_recv()

    def rows_of(h):
        return pl.ds(h * HROWS, HROWS)

    load_ids = load(ids_hbm, ids, 0)
    load_srv = load(srv_hbm, srv, 1)
    load_t = load(t_hbm, tv, 2)
    load_h = [load(hid.at[rows_of(h)], h_all.at[h, gi], 3 + h) for h in range(2)]
    load_w = load(w_hbm, w, 5)

    load_ids.wait()
    load_srv.wait()
    pt[...] = (lax.broadcasted_iota(I32, (ROWS, ROWS), 0) == srv[...]).astype(BF16)
    ids_all[gi] = ids[...]
    for cp in load_h:
        cp.wait()

    pl.semaphore_wait(bar, len(peers))

    ycols = pl.ds(pl.multiple_of(y * YW, 128), YW)
    zcols = pl.ds(pl.multiple_of(ZB + z * ZW, ZW), ZW)
    cross_y, cross_z = [], []
    for h in range(2):
        for cols, cps in ((zcols, cross_z), (ycols, cross_y)):
            piece = h_all.at[h, gi, :, cols]
            cps.append(send(piece, piece, partner))
    pair = [send(h_all.at[h, gi], h_all.at[h, gi], other) for h in range(2)]
    idc = [send(ids_all.at[gi], ids_all.at[gi], (lax.rem(gi + k, GRPS), vi)) for k in range(1, GRPS)]

    load_t.wait()
    for q in range(GRPS):
        tst[q] = tv[:, q, :]
    t_all = tst[...].astype(F32)
    tm = jnp.max(jnp.max(t_all, axis=0), axis=1, keepdims=True)
    tsum = jnp.sum(jnp.sum(jnp.exp((t_all - tm[None]) * 0.5), axis=0), axis=1, keepdims=True)
    lse = jnp.broadcast_to(tm * 0.5 + jnp.log(tsum), (GROWS, 128)).T[0:1, :]
    none = jnp.full((1, GROWS), -1e30, F32)
    for j in range(GRPS):
        sta[0, 3 + j // 2 : 4 + j // 2, (j % 2) * GROWS : (j % 2 + 1) * GROWS] = jnp.where(gi == j, lse, none)

    gg = 2 * (1 - xh) + c
    fwd_y, fwd_z = [], []

    def forward(h):
        cross_z[h].wait_recv()
        piece = h_all.at[h, gg, :, zcols]
        fwd_z.append([send(piece, piece, p) for p in zs])
        cross_y[h].wait_recv()
        piece = h_all.at[h, gg, :, ycols]
        fwd_y.append([send(piece, piece, p) for p in ys])

    def share(h):
        cps = []
        for fwd, cols in ((fwd_y, pl.ds(0, ZB)), (fwd_z, pl.ds(ZB, NZ * ZW))):
            await_all(fwd[h])
            piece = h_all.at[h, gg, :, cols]
            cps.append(send(piece, piece, other))
        return cps

    def two_groups(part):
        return pl.ds(pl.multiple_of(part * GROWS, GROWS), GROWS)

    def logits(h, part):
        a = h_all[h, pl.ds(2 * part, 2)].reshape(GROWS, DS)
        lg[h, two_groups(part), :] = jnp.dot(a, w[...], preferred_element_type=F32)

    def student_stats(h, part):
        r = two_groups(part)
        l = lg[h, r, :]
        m = jnp.max(l, axis=1, keepdims=True)
        e = jnp.exp((l - m) * 0.5)
        lg[h, r, :] = e
        lane = lax.broadcasted_iota(I32, (GROWS, 128), 1)
        hard = jnp.sum(e * e, axis=1, keepdims=True)
        soft = jnp.sum(e, axis=1, keepdims=True)
        stc[h, r, :] = jnp.where(lane == 0, m, jnp.where(lane == 1, hard, soft))

    def turn_rows(h, part):
        cols = pl.ds(pl.multiple_of(h * HALF + part * GROWS, GROWS), GROWS)

        def step(i, _):
            s = pl.ds(pl.multiple_of(i * HW, HW), HW)
            ht[s, cols] = h_all[h, pl.ds(2 * part, 2), :, s].reshape(GROWS, HW).T
            return 0

        lax.fori_loop(0, HCH, step, 0)

    forward(0)
    load_w.wait()
    await_all(pair)
    logits(0, xh)
    forward(1)
    teach = []
    for k in range(1, GRPS):
        q = lax.rem(gi + k, GRPS)
        teach.append(send(tst.at[q], tall.at[gi], (q, vi)))
    tall[gi] = tst[gi]
    logits(1, xh)
    student_stats(0, xh)

    st = [sta, stb]
    st_c = [sta_c, stb_c]
    st_x = [sta_x, stb_x]
    st_y = [sta_y, stb_y]
    st_z = [sta_z, stb_z]

    def stats_begin(h):
        for j in range(2):
            s = slice(j * 128, (j + 1) * 128)
            st[h][0, 0:3, s] = stc[h, s, :].T[0:3, :]
        return [send(st[h].at[0], st_c[h], other)]

    def stats_x(h, cps):
        await_all(cps)
        put(st[h].at[1], merge([st[h][0], st_c[h][...]]))
        return [send(st[h].at[1], st_x[h].at[k], p) for k, p in enumerate(xs)]

    def stats_y(h, cps):
        await_all(cps)
        put(st[h].at[2], merge([st[h][1], *[st_x[h][k] for k in range(NX - 1)]]))
        return [send(st[h].at[2], st_y[h].at[k], p) for k, p in enumerate(ys)]

    def stats_z(h, cps):
        await_all(cps)
        put(st[h].at[3], merge([st[h][2], *[st_y[h][k] for k in range(NY - 1)]]))
        return [send(st[h].at[3], st_z[h].at[k], p) for k, p in enumerate(zs)]

    def stats_end(h, cps):
        await_all(cps)
        ms, hard, soft, *lse = merge([st[h][3], *[st_z[h][k] for k in range(NZ - 1)]])
        d = jnp.exp((st[h][0, 0:1, :] - ms) * 0.5)
        fin[0:1, :] = 32.0 * d / soft
        fin[1:2, :] = 16.0 * d * d / hard
        for j in range(2):
            s = slice(j * 128, (j + 1) * 128)
            fint[h, s, :] = fin[:, s].T
        return lse

    def turn_w(first, last):
        def step(i, _):
            s = pl.ds(pl.multiple_of(i * HW, HW), HW)
            wt[:, s] = w[s, :].T
            return 0

        lax.fori_loop(first, last, step, 0)

    def make_perm():
        i = lax.broadcasted_iota(I32, (HALF, 1), 0)
        i_c, hi, lo = lax.div(i, 128), lax.rem(lax.div(i, 32), 4), lax.rem(lax.div(i, 8), 4)
        i_z, i_b = lax.rem(lax.div(i, 2), 4), lax.rem(i, 2)
        col = lax.broadcasted_iota(I32, (HALF, HALF), 1)
        for p, (i_x, i_y) in enumerate(((hi, lo), (lo, hi))):
            r = (2 * lax.div(i_x, 2) + i_c) * HROWS + i_z * 16 + lax.rem(i_x, 2) * 8 + i_y * 2 + i_b
            perm[p] = (col == r).astype(BF16)

    fin[...] = jnp.zeros_like(fin)
    rowf[...] = jnp.zeros_like(rowf)
    shared = [share(0)]
    student_stats(1, xh)
    await_all(shared[0])
    logits(0, 1 - xh)
    student_stats(0, 1 - xh)
    m0 = stats_begin(0)
    shared.append(share(1))
    m0 = stats_x(0, m0)
    await_all(shared[1])
    logits(1, 1 - xh)
    student_stats(1, 1 - xh)
    m1 = stats_begin(1)
    m0 = stats_y(0, m0)
    m1 = stats_x(1, m1)
    make_perm()
    turn_w(0, 3)
    m0 = stats_z(0, m0)
    m1 = stats_y(1, m1)
    turn_w(3, HCH)

    await_all(teach)
    al[...] = lax.dot_general(
        pt[...], tall[...].reshape(ROWS, COLS), (((0,), (0,)), ((), ())), preferred_element_type=F32
    )
    await_all(idc)
    for j in range(GRPS):
        rowf[0:1, j * 128 : (j + 1) * 128] = ids_all[j].astype(F32)
    (lse,) = stats_end(0, m0)
    terms = 0.0
    for j in range(2):
        part = lse[j : j + 1, :]
        for k in range(3):
            term = part.astype(BF16).astype(F32)
            rowf[8 + k : 9 + k, j * HALF : (j + 1) * HALF] = term
            part = part - term
    terms = jnp.dot(rowf[8:16, :].astype(BF16), pt[...], preferred_element_type=F32)
    rowf[1:2, :] = terms[0:1] + terms[1:2] + terms[2:3]
    for j in range(4):
        s = slice(j * 128, (j + 1) * 128)
        rowt[s, :] = rowf[:, s].T

    first = (gi * (NX // 2 * NY * NZ) + vi) * COLS

    def grad(h):
        def step(j, _):
            r = pl.ds(pl.multiple_of(j * HROWS, HROWS), HROWS)
            full = pl.ds(pl.multiple_of(j * GROWS + h * HROWS, HROWS), HROWS)
            f = fint[h, r, :]
            f2 = rowt[full, :]
            e = lg[h, r, :]
            col = lax.broadcasted_iota(I32, (HROWS, COLS), 1) + first
            hit = jnp.where(f2[:, 0:1].astype(I32) == col, 16.0, 0.0)
            soft = e * f[:, 0:1] - 32.0 * jnp.exp(al[full, :] * 0.5 - f2[:, 1:2])
            g[pl.ds(pl.multiple_of(h * HALF + j * HROWS, HROWS), HROWS), :] = (
                soft + (e * e * f[:, 1:2] - hit)
            ).astype(BF16)
            return 0

        lax.fori_loop(0, GRPS, step, 0)
        for p in range(2):
            gp[p] = jnp.dot(perm[p], g[h * HALF : (h + 1) * HALF, :], preferred_element_type=F32).astype(BF16)

    def pair_stage(h):
        cps = []
        for p in range(2):
            s = slice(p * CW, (p + 1) * CW)
            t = jnp.dot(gp[p, two_groups(1 - c), :], wt[:, s], preferred_element_type=F32)
            dsend[h, p] = t.astype(BF16).reshape(4, 32, CW)
            cps.append(send(dsend.at[h, p], drecv.at[h, p], other))
        for p in range(2):
            s = slice(p * CW, (p + 1) * CW)
            t = jnp.dot(gp[p, two_groups(c), :], wt[:, s], preferred_element_type=F32)
            own[h, p] = t.reshape(4, 32, CW)
        return cps

    x_side = 2 * xh + 1 - xl
    y_side = y + 1 - 2 * lax.rem(y, 2)
    axes = [
        (x, ((3 - x, partner), (x_side, device(x_side, y, z, c))), y, ys),
        (y, ((3 - y, device(x, 3 - y, z, c)), (y_side, device(x, y_side, z, c))), x, xs),
    ]
    subs = (slice(0, CW // 2), slice(CW // 2, CW))

    def chip_sum(h, p, k, cols):
        return own[h, p, k, :, cols] + drecv[h, p, k, :, cols].astype(F32)

    def first_stage(h, p, cp):
        cp.wait_recv()
        me, sides, _, _ = axes[p]
        opposite = lax.rem(me + 2, 4)
        cps = []
        for i, cols in enumerate(subs):
            place, to = sides[i]
            s1[h, p, i, 0] = chip_sum(h, p, place, cols).astype(BF16)
            s1[h, p, i, 1] = chip_sum(h, p, opposite, cols).astype(BF16)
            cps.append(send(s1.at[h, p, i], r1.at[h, p, i], to))
        return cps

    def first_stage_end(h, p, cps):
        sides = axes[p][1]
        out = []
        for i, cols in enumerate(subs):
            cps[i].wait_recv()
            place, to = sides[1 - i]
            s1b[h, p, i] = (chip_sum(h, p, place, cols) + r1[h, p, i, 1].astype(F32)).astype(BF16)
            out.append(send(s1b.at[h, p, i], r1b.at[h, p, i], to))
        return out

    def second_stage(h, p, cps):
        await_all(cps)
        me, _, me2, to = axes[p]
        t = [chip_sum(h, p, me, cols) + (r1[h, p, i, 0].astype(F32) + r1b[h, p, i].astype(F32)) for i, cols in enumerate(subs)]
        for j in range(4):
            r = slice(j * 8, (j + 1) * 8)
            acc[h, p, j, :, subs[0]] = t[0][r]
            acc[h, p, j, :, subs[1]] = t[1][r]
            s2[h, p, j] = jnp.concatenate([t[0][r], t[1][r]], axis=0).astype(BF16)
        return [send(s2.at[h, p, lax.rem(me2 + k, 4)], r2.at[h, p, k - 1], d) for k, d in enumerate(to, 1)]

    base3 = 100
    s3f[:, 14:16, :] = jnp.zeros((NZ, 2, 512), F32)

    def third_copy(k, to):
        return pltpu.make_async_remote_copy(
            src_ref=s3.at[to],
            dst_ref=r3.at[k - 1],
            send_sem=ssem.at[base3 + k],
            recv_sem=rsem.at[base3 + k],
            device_id=device(x, y, to, c),
            device_id_type=MESH,
        )

    def third_stage(h, parts):
        for p, cps in enumerate(parts):
            await_all(cps)
            t = acc[h, p, axes[p][2]]
            u = r2[h, p, 0].astype(F32) + r2[h, p, 1].astype(F32) + r2[h, p, 2].astype(F32)
            base = p * CW
            acc3[:, base : base + CW // 2] = t[:, : CW // 2] + u[0:8]
            acc3[:, base + CW // 2 : base + CW] = t[:, CW // 2 :] + u[8:16]
        for j in range(4):
            for k in range(DS // 512):
                s3f[4 * h + j, 2 * k : 2 * k + 2, :] = acc3[2 * j : 2 * j + 2, k * 512 : (k + 1) * 512]
            s3[4 * h + j] = s3f[4 * h + j].astype(BF16)
        for k in range(1, NZ):
            to = lax.rem(z + k, NZ)

            @pl.when(lax.div(to, 4) == h)
            def _():
                third_copy(k, to).start()

    def third_end():
        for k in range(1, NZ):
            third_copy(k, lax.rem(z + k, NZ)).wait_recv()
        t = s3f[z]
        for k in range(NZ - 1):
            t = t + r3[k].astype(F32)
        for k in range(DS // 512):
            gh_out[:, k * 512 : (k + 1) * 512] = t[2 * k : 2 * k + 2, :]
        for k in range(1, NZ):
            third_copy(k, lax.rem(z + k, NZ)).wait_send()

    def head(first, last):
        def step(k, _):
            s = pl.ds(pl.multiple_of(k * HW, HW), HW)
            ghead_out[s, :] = jnp.dot(ht[s, :], g[...], preferred_element_type=F32).astype(BF16)
            return 0

        lax.fori_loop(first, last, step, 0)

    grad(0)
    m1 = stats_z(1, m1)
    a0, b0 = pair_stage(0)
    a0 = first_stage(0, 0, a0)
    b0 = first_stage(0, 1, b0)
    stats_end(1, m1)
    grad(1)
    a1, b1 = pair_stage(1)
    a0 = first_stage_end(0, 0, a0)
    b0 = first_stage_end(0, 1, b0)
    a1 = first_stage(1, 0, a1)
    b1 = first_stage(1, 1, b1)
    for h in range(2):
        turn_rows(h, xh)
    a0 = second_stage(0, 0, a0)
    b0 = second_stage(0, 1, b0)
    a1 = first_stage_end(1, 0, a1)
    b1 = first_stage_end(1, 1, b1)
    for h in range(2):
        turn_rows(h, 1 - xh)
    head(0, 2)
    third_stage(0, (a0, b0))
    a1 = second_stage(1, 0, a1)
    b1 = second_stage(1, 1, b1)
    head(2, HCH)
    third_stage(1, (a1, b1))
    third_end()

    for cp in started:
        cp.wait_send()


def write_out(sums, head, gh_out, ghead_out, sem):
    cps = [pltpu.make_async_copy(sums, gh_out, sem.at[HCH])]
    for k in range(HCH):
        s = pl.ds(k * HW, HW)
        cps.append(pltpu.make_async_copy(head.at[s], ghead_out.at[s], sem.at[k]))
    for cp in cps:
        cp.start()
    for cp in cps:
        cp.wait()


N_SEMS = 112


def body(hidden, token_ids, serving, head_weight, teacher_logits):
    vm = pltpu.VMEM
    sums, head = pl.pallas_call(
        kernel,
        out_shape=(
            vm((2, DS), F32),
            vm((DS, COLS), BF16),
        ),
        in_specs=[pl.BlockSpec(memory_space=pltpu.HBM)] * 5,
        out_specs=(pl.BlockSpec(memory_space=vm), pl.BlockSpec(memory_space=vm)),
        scratch_shapes=[
            vm((1, GROWS), I32),
            vm((1, ROWS), I32),
            vm((2, GRPS, HROWS, DS), BF16),
            vm((DS, COLS), BF16),
            vm((COLS, DS), BF16),
            vm((DS, ROWS), BF16),
            vm((GROWS, GRPS, COLS), BF16),
            vm((GRPS, GROWS, COLS), BF16),
            vm((GRPS, GROWS, COLS), BF16),
            vm((GRPS, 1, GROWS), I32),
            vm((ROWS, ROWS), BF16),
            vm((2, HALF, HALF), BF16),
            vm((2, HALF, COLS), F32),
            vm((ROWS, COLS), F32),
            vm((2, HALF, 128), F32),
            vm((4, 8, HALF), F32),
            vm((8, HALF), F32),
            vm((NX - 1, 8, HALF), F32),
            vm((NY - 1, 8, HALF), F32),
            vm((NZ - 1, 8, HALF), F32),
            vm((4, 4, HALF), F32),
            vm((4, HALF), F32),
            vm((NX - 1, 4, HALF), F32),
            vm((NY - 1, 4, HALF), F32),
            vm((NZ - 1, 4, HALF), F32),
            vm((128, HALF), F32),
            vm((2, HALF, 128), F32),
            vm((128, ROWS), F32),
            vm((ROWS, 128), F32),
            vm((ROWS, COLS), BF16),
            vm((2, HALF, COLS), BF16),
            vm((2, 2, 4, 32, CW), F32),
            vm((2, 2, 4, 32, CW), BF16),
            vm((2, 2, 4, 32, CW), BF16),
            vm((2, 2, 2, 2, 32, CW // 2), BF16),
            vm((2, 2, 2, 2, 32, CW // 2), BF16),
            vm((2, 2, 2, 32, CW // 2), BF16),
            vm((2, 2, 2, 32, CW // 2), BF16),
            vm((2, 2, 4, 8, CW), F32),
            vm((2, 2, 4, 16, CW // 2), BF16),
            vm((2, 2, 3, 16, CW // 2), BF16),
            vm((8, DS), F32),
            vm((NZ, 16, 512), F32),
            vm((NZ, 16, 512), BF16),
            vm((NZ - 1, 16, 512), BF16),
            pltpu.SemaphoreType.DMA((N_SEMS,)),
            pltpu.SemaphoreType.DMA((N_SEMS,)),
            pltpu.SemaphoreType.DMA((6,)),
        ],
        compiler_params=pltpu.CompilerParams(
            collective_id=0, has_side_effects=True, vmem_limit_bytes=48 * 1024 * 1024
        ),
        name="distill_backward",
    )(*[
        pltpu.with_memory_space_constraint(a, pltpu.HBM)
        for a in (hidden, token_ids.reshape(1, GROWS), serving.reshape(1, ROWS), head_weight, teacher_logits)
    ])
    return pl.pallas_call(
        write_out,
        out_shape=(
            jax.ShapeDtypeStruct((2, DS), F32),
            jax.ShapeDtypeStruct((DS, COLS), BF16),
        ),
        in_specs=[pl.BlockSpec(memory_space=vm)] * 2,
        out_specs=(pl.BlockSpec(memory_space=pl.ANY), pl.BlockSpec(memory_space=pl.ANY)),
        scratch_shapes=[pltpu.SemaphoreType.DMA((1 + HCH,))],
        compiler_params=pltpu.CompilerParams(vmem_limit_bytes=1024 * 1024),
        name="write_out",
    )(sums, head)


def solution(mesh):
    placed = (P("grp", None), P("grp"), P(), P(None, ("grp", "vocab")), P("grp", None, "vocab"))
    return jax.shard_map(
        body,
        mesh=mesh,
        in_specs=placed,
        out_specs=(P(("grp", "vocab"), None), P(None, ("grp", "vocab"))),
        check_vma=False,
    )
```

time: 497 us -> 65.8 us (0.13)
  waiting for transfers between devices: 284 us -> 0 us
  blocking collectives: 162 us -> 0 us
  Pallas kernels: 0 us -> 65.1 us
  matrix products: 19.5 us -> 0 us
  between operations: 14.1 us -> 0.64 us
  local copies, waits for them, and re-layouts: 11.5 us -> 0 us
    unnamed x3 -> x0, waiting for transfers between devices: 261 us -> none
    pmax x1 -> x0, blocking collectives: 76.9 us -> none  [body(): lax.pmax((local_peak, local_tpeak), ('grp', 'vocab'))]
    psum x1 -> x0, blocking collectives: 74.3 us -> none  [body(): lax.psum((jnp.sum(jnp.exp(shifted_pupil_activations), axis=1), jnp.sum(jn...]
    pallas_call x0 -> x2, Pallas kernels: none -> 65.1 us  [the longest x1 63.2 us: body(): pl.pallas_call(kernel, out_shape=(vm((2, DS), F32), vm((DS, COLS), BF16))...]
    all_gather x1 -> x0, waiting for transfers between devices: 22.4 us -> none  [body(): lax.all_gather(hidden, 'grp', axis=0, tiled=True)]
    dot_general x3 -> x0, matrix products: 19.5 us -> none  [the longest x1 7.74 us: body(): lax.dot_general(activation_derivative, head_weight, (((1,), (1,)), ((), (...]
    all_gather x1 -> x0, blocking collectives: 11.1 us -> none  [body(): lax.all_gather(token_ids, 'grp', axis=0, tiled=True)]
    unnamed x3 -> x0, local copies, waits for them, and re-layouts: 9.36 us -> none
  transfers between devices with their start and end apart: 3 -> 0, of which waited for: 2 -> 0; matrix products, arithmetic and copies ran while one was open for 4% -> 0% of each run, Pallas kernels for 0% -> 0%
where the time goes in v3:
time: 65.8 us; the launch traced here: 65.7 us
  Pallas kernels  65.1 us (99%)
    pallas_call x1, Pallas kernels, body(): pl.pallas_call(kernel, out_shape=(vm((2, DS), F32), vm((DS, COLS), BF16))...  63.2 us
    pallas_call x1, Pallas kernels, body(): pl.pallas_call(write_out, out_shape=(jax.ShapeDtypeStruct((2, DS), F32),...  1.91 us

profile of v3, /device:TPU:2, one launch (start us, length us, event | category | flops | bytes accessed | tf_op | source)
XLA Modules:
  0.0 65.7 jit_solution(3694749698654015065)
XLA Ops:
  0.6 63.2 %distill_backward.1 = (f32[2,3584]{1,0:T(2,128)S(1)}, bf16[3584,512]{1,0:T(8,128)(2,1)S(1)}) custom-call(bf16[128,3584]{1,0:T(8,128)(2,1)} %hid.1, s32[1,128]{1,0:T(1,128)} %bitcast.3, s32[1,512]{1,0:T(1,128)} %bitcast.2, bf16[3584,512]{1,0:T(8,128)(2,1)} %w_hbm.1, bf16[128,4,512]{2,1,0:T(4,128)(2,1)} %t_hbm.1), custom_call_target="tpu_custom_call" | custom-call | tf_op jit(solution)/shard_map/distill_backward/pallas_call | solution.py:485
  63.8 1.9 %write_out.1 = (f32[2,3584]{1,0:T(2,128)}, bf16[3584,512]{1,0:T(8,128)(2,1)}) custom-call(f32[2,3584]{1,0:T(2,128)S(1)} %get-tuple-element.4.sums, bf16[3584,512]{1,0:T(8,128)(2,1)S(1)} %get-tuple-element.5.head), custom_call_target="tpu_custom_call" | custom-call | tf_op jit(solution)/shard_map/write_out/pallas_call | solution.py:551

commit v4 on v3

--- a/solution.py
+++ b/solution.py
@@ -27,6 +27,7 @@
 ZB = NY * YW
 
 CW = DS // 2
+SW = CW // 2
 
 HCH = 7
 HW = DS // HCH
@@ -62,7 +63,7 @@
 def kernel(
     hid, ids_hbm, srv_hbm, w_hbm, t_hbm, gh_out, ghead_out,
     ids, srv, h_all, w, wt, ht, tv, tst, tall, ids_all, pt, perm, lg, al, stc,
-    sta, sta_c, sta_x, sta_y, sta_z, stb, stb_c, stb_x, stb_y, stb_z,
+    sta, sta_x, sta_y, sta_z, stb, stb_x, stb_y, stb_z,
     fin, fint, rowf, rowt, g, gp, own, dsend, drecv, s1, r1, s1b, r1b, acc, s2, r2, acc3, s3f, s3, r3,
     ssem, rsem, lsem,
 ):
@@ -79,10 +80,10 @@
     xs = [device(lax.rem(x + k, NX), y, z, c) for k in range(1, NX)]
     ys = [device(x, lax.rem(y + k, NY), z, c) for k in range(1, NY)]
     zs = [device(x, y, lax.rem(z + k, NZ), c) for k in range(1, NZ)]
-    far = device(lax.rem(x + 2, NX), y, z, 1 - c)
+    xos = [device(lax.rem(x + k, NX), y, z, 1 - c) for k in range(1, NX)]
 
     bar = pltpu.get_barrier_semaphore()
-    peers = [other, *xs, *ys, *zs, far]
+    peers = [other, *xs, *xos, *ys, *zs]
     for p in peers:
         pl.semaphore_signal(bar, inc=1, device_id=p, device_id_type=MESH)
 
@@ -208,25 +209,19 @@
     student_stats(0, xh)
 
     st = [sta, stb]
-    st_c = [sta_c, stb_c]
     st_x = [sta_x, stb_x]
     st_y = [sta_y, stb_y]
     st_z = [sta_z, stb_z]
 
-    def stats_begin(h):
+    def stats_x(h):
         for j in range(2):
             s = slice(j * 128, (j + 1) * 128)
             st[h][0, 0:3, s] = stc[h, s, :].T[0:3, :]
-        return [send(st[h].at[0], st_c[h], other)]
-
-    def stats_x(h, cps):
-        await_all(cps)
-        put(st[h].at[1], merge([st[h][0], st_c[h][...]]))
-        return [send(st[h].at[1], st_x[h].at[k], p) for k, p in enumerate(xs)]
+        return [send(st[h].at[0], st_x[h].at[k], p) for k, p in enumerate([*xs, *xos, other])]
 
     def stats_y(h, cps):
         await_all(cps)
-        put(st[h].at[2], merge([st[h][1], *[st_x[h][k] for k in range(NX - 1)]]))
+        put(st[h].at[2], merge([st[h][0], *[st_x[h][k] for k in range(2 * NX - 1)]]))
         return [send(st[h].at[2], st_y[h].at[k], p) for k, p in enumerate(ys)]
 
     def stats_z(h, cps):
@@ -269,15 +264,13 @@
     await_all(shared[0])
     logits(0, 1 - xh)
     student_stats(0, 1 - xh)
-    m0 = stats_begin(0)
+    m0 = stats_x(0)
     shared.append(share(1))
-    m0 = stats_x(0, m0)
     await_all(shared[1])
     logits(1, 1 - xh)
     student_stats(1, 1 - xh)
-    m1 = stats_begin(1)
+    m1 = stats_x(1)
     m0 = stats_y(0, m0)
-    m1 = stats_x(1, m1)
     make_perm()
     turn_w(0, 3)
     m0 = stats_z(0, m0)
@@ -291,6 +284,7 @@
     await_all(idc)
     for j in range(GRPS):
         rowf[0:1, j * 128 : (j + 1) * 128] = ids_all[j].astype(F32)
+    m1 = stats_z(1, m1)
     (lse,) = stats_end(0, m0)
     terms = 0.0
     for j in range(2):
@@ -326,17 +320,17 @@
         for p in range(2):
             gp[p] = jnp.dot(perm[p], g[h * HALF : (h + 1) * HALF, :], preferred_element_type=F32).astype(BF16)
 
+    pieces = [(p, i) for i in range(2) for p in range(2)]
+
+    def partial(p, i, core):
+        s = slice((2 * p + i) * SW, (2 * p + i + 1) * SW)
+        return jnp.dot(gp[p, two_groups(core), :], wt[:, s], preferred_element_type=F32)
+
     def pair_stage(h):
-        cps = []
-        for p in range(2):
-            s = slice(p * CW, (p + 1) * CW)
-            t = jnp.dot(gp[p, two_groups(1 - c), :], wt[:, s], preferred_element_type=F32)
-            dsend[h, p] = t.astype(BF16).reshape(4, 32, CW)
-            cps.append(send(dsend.at[h, p], drecv.at[h, p], other))
-        for p in range(2):
-            s = slice(p * CW, (p + 1) * CW)
-            t = jnp.dot(gp[p, two_groups(c), :], wt[:, s], preferred_element_type=F32)
-            own[h, p] = t.reshape(4, 32, CW)
+        cps = {}
+        for p, i in pieces:
+            dsend[h, p, i] = partial(p, i, 1 - c).astype(BF16).reshape(4, 32, SW)
+            cps[p, i] = send(dsend.at[h, p, i], drecv.at[h, p, i], other)
         return cps
 
     x_side = 2 * xh + 1 - xl
@@ -345,45 +339,48 @@
         (x, ((3 - x, partner), (x_side, device(x_side, y, z, c))), y, ys),
         (y, ((3 - y, device(x, 3 - y, z, c)), (y_side, device(x, y_side, z, c))), x, xs),
     ]
-    subs = (slice(0, CW // 2), slice(CW // 2, CW))
-
-    def chip_sum(h, p, k, cols):
-        return own[h, p, k, :, cols] + drecv[h, p, k, :, cols].astype(F32)
-
-    def first_stage(h, p, cp):
-        cp.wait_recv()
-        me, sides, _, _ = axes[p]
-        opposite = lax.rem(me + 2, 4)
-        cps = []
-        for i, cols in enumerate(subs):
+
+    def chip_sum(h, p, i, k):
+        return own[h, p, i, k] + drecv[h, p, i, k].astype(F32)
+
+    def first_stage(h, cps):
+        out = {}
+        for p, i in pieces:
+            own[h, p, i] = partial(p, i, c).reshape(4, 32, SW)
+            cps[p, i].wait_recv()
+            me, sides, _, _ = axes[p]
             place, to = sides[i]
-            s1[h, p, i, 0] = chip_sum(h, p, place, cols).astype(BF16)
-            s1[h, p, i, 1] = chip_sum(h, p, opposite, cols).astype(BF16)
-            cps.append(send(s1.at[h, p, i], r1.at[h, p, i], to))
-        return cps
-
-    def first_stage_end(h, p, cps):
-        sides = axes[p][1]
+            s1[h, p, i, 0] = chip_sum(h, p, i, place).astype(BF16)
+            s1[h, p, i, 1] = chip_sum(h, p, i, lax.rem(me + 2, 4)).astype(BF16)
+            out[p, i] = send(s1.at[h, p, i], r1.at[h, p, i], to)
+        return out
+
+    def first_stage_end(h, cps):
+        out = {}
+        for p, i in pieces:
+            cps[p, i].wait_recv()
+            place, to = axes[p][1][1 - i]
+            s1b[h, p, i] = (chip_sum(h, p, i, place) + r1[h, p, i, 1].astype(F32)).astype(BF16)
+            out[p, i] = send(s1b.at[h, p, i], r1b.at[h, p, i], to)
+        return out
+
+    def second_stage(h, cps):
         out = []
-        for i, cols in enumerate(subs):
-            cps[i].wait_recv()
-            place, to = sides[1 - i]
-            s1b[h, p, i] = (chip_sum(h, p, place, cols) + r1[h, p, i, 1].astype(F32)).astype(BF16)
-            out.append(send(s1b.at[h, p, i], r1b.at[h, p, i], to))
+        for p in range(2):
+            await_all([cps[p, 0], cps[p, 1]])
+            me, _, me2, to = axes[p]
+            t = [
+                chip_sum(h, p, i, me) + (r1[h, p, i, 0].astype(F32) + r1b[h, p, i].astype(F32)) for i in range(2)
+            ]
+            for j in range(4):
+                r = slice(j * 8, (j + 1) * 8)
+                acc[h, p, j, :, :SW] = t[0][r]
+                acc[h, p, j, :, SW:] = t[1][r]
+                s2[h, p, j] = jnp.concatenate([t[0][r], t[1][r]], axis=0).astype(BF16)
+            out.append([send(s2.at[h, p, lax.rem(me2 + k, 4)], r2.at[h, p, k - 1], d) for k, d in enumerate(to, 1)])
         return out
 
-    def second_stage(h, p, cps):
-        await_all(cps)
-        me, _, me2, to = axes[p]
-        t = [chip_sum(h, p, me, cols) + (r1[h, p, i, 0].astype(F32) + r1b[h, p, i].astype(F32)) for i, cols in enumerate(subs)]
-        for j in range(4):
-            r = slice(j * 8, (j + 1) * 8)
-            acc[h, p, j, :, subs[0]] = t[0][r]
-            acc[h, p, j, :, subs[1]] = t[1][r]
-            s2[h, p, j] = jnp.concatenate([t[0][r], t[1][r]], axis=0).astype(BF16)
-        return [send(s2.at[h, p, lax.rem(me2 + k, 4)], r2.at[h, p, k - 1], d) for k, d in enumerate(to, 1)]
-
-    base3 = 100
+    base3 = 120
     s3f[:, 14:16, :] = jnp.zeros((NZ, 2, 512), F32)
 
     def third_copy(k, to):
@@ -402,8 +399,8 @@
             t = acc[h, p, axes[p][2]]
             u = r2[h, p, 0].astype(F32) + r2[h, p, 1].astype(F32) + r2[h, p, 2].astype(F32)
             base = p * CW
-            acc3[:, base : base + CW // 2] = t[:, : CW // 2] + u[0:8]
-            acc3[:, base + CW // 2 : base + CW] = t[:, CW // 2 :] + u[8:16]
+            acc3[:, base : base + SW] = t[:, : SW] + u[0:8]
+            acc3[:, base + SW : base + CW] = t[:, SW :] + u[8:16]
         for j in range(4):
             for k in range(DS // 512):
                 s3f[4 * h + j, 2 * k : 2 * k + 2, :] = acc3[2 * j : 2 * j + 2, k * 512 : (k + 1) * 512]
@@ -435,31 +432,24 @@
         lax.fori_loop(first, last, step, 0)
 
     grad(0)
-    m1 = stats_z(1, m1)
-    a0, b0 = pair_stage(0)
-    a0 = first_stage(0, 0, a0)
-    b0 = first_stage(0, 1, b0)
+    m0 = pair_stage(0)
+    m0 = first_stage(0, m0)
     stats_end(1, m1)
     grad(1)
-    a1, b1 = pair_stage(1)
-    a0 = first_stage_end(0, 0, a0)
-    b0 = first_stage_end(0, 1, b0)
-    a1 = first_stage(1, 0, a1)
-    b1 = first_stage(1, 1, b1)
+    m1 = pair_stage(1)
+    m0 = first_stage_end(0, m0)
+    m1 = first_stage(1, m1)
     for h in range(2):
         turn_rows(h, xh)
-    a0 = second_stage(0, 0, a0)
-    b0 = second_stage(0, 1, b0)
-    a1 = first_stage_end(1, 0, a1)
-    b1 = first_stage_end(1, 1, b1)
+    m0 = second_stage(0, m0)
+    m1 = first_stage_end(1, m1)
     for h in range(2):
         turn_rows(h, 1 - xh)
     head(0, 2)
-    third_stage(0, (a0, b0))
-    a1 = second_stage(1, 0, a1)
-    b1 = second_stage(1, 1, b1)
+    third_stage(0, m0)
+    m1 = second_stage(1, m1)
     head(2, HCH)
-    third_stage(1, (a1, b1))
+    third_stage(1, m1)
     third_end()
 
     for cp in started:
@@ -477,7 +467,7 @@
         cp.wait()
 
 
-N_SEMS = 112
+N_SEMS = 128
 
 
 def body(hidden, token_ids, serving, head_weight, teacher_logits):
@@ -507,13 +497,11 @@
             vm((ROWS, COLS), F32),
             vm((2, HALF, 128), F32),
             vm((4, 8, HALF), F32),
-            vm((8, HALF), F32),
-            vm((NX - 1, 8, HALF), F32),
+            vm((2 * NX - 1, 8, HALF), F32),
             vm((NY - 1, 8, HALF), F32),
             vm((NZ - 1, 8, HALF), F32),
             vm((4, 4, HALF), F32),
-            vm((4, HALF), F32),
-            vm((NX - 1, 4, HALF), F32),
+            vm((2 * NX - 1, 4, HALF), F32),
             vm((NY - 1, 4, HALF), F32),
             vm((NZ - 1, 4, HALF), F32),
             vm((128, HALF), F32),
@@ -522,16 +510,16 @@
             vm((ROWS, 128), F32),
             vm((ROWS, COLS), BF16),
             vm((2, HALF, COLS), BF16),
-            vm((2, 2, 4, 32, CW), F32),
-            vm((2, 2, 4, 32, CW), BF16),
-            vm((2, 2, 4, 32, CW), BF16),
-            vm((2, 2, 2, 2, 32, CW // 2), BF16),
-            vm((2, 2, 2, 2, 32, CW // 2), BF16),
-            vm((2, 2, 2, 32, CW // 2), BF16),
-            vm((2, 2, 2, 32, CW // 2), BF16),
+            vm((2, 2, 2, 4, 32, SW), F32),
+            vm((2, 2, 2, 4, 32, SW), BF16),
+            vm((2, 2, 2, 4, 32, SW), BF16),
+            vm((2, 2, 2, 2, 32, SW), BF16),
+            vm((2, 2, 2, 2, 32, SW), BF16),
+            vm((2, 2, 2, 32, SW), BF16),
+            vm((2, 2, 2, 32, SW), BF16),
             vm((2, 2, 4, 8, CW), F32),
-            vm((2, 2, 4, 16, CW // 2), BF16),
-            vm((2, 2, 3, 16, CW // 2), BF16),
+            vm((2, 2, 4, 16, SW), BF16),
+            vm((2, 2, 3, 16, SW), BF16),
             vm((8, DS), F32),
             vm((NZ, 16, 512), F32),
             vm((NZ, 16, 512), BF16),

time: 65.8 us -> 64.2 us (0.976); the launches traced: 65.7 us -> 63.2 us
  Pallas kernels: 65.1 us -> 62.6 us
    pallas_call x1, Pallas kernels: 63.2 us -> 60.7 us  [body(): pl.pallas_call(kernel, out_shape=(vm((2, DS), F32), vm((DS, COLS), BF16))...]
where the time goes in v4:
time: 64.2 us; the launch traced here: 63.2 us
  Pallas kernels  62.6 us (98%)
    pallas_call x1, Pallas kernels, body(): pl.pallas_call(kernel, out_shape=(vm((2, DS), F32), vm((DS, COLS), BF16))...  60.7 us
    pallas_call x1, Pallas kernels, body(): pl.pallas_call(write_out, out_shape=(jax.ShapeDtypeStruct((2, DS), F32),...  1.91 us

profile of v4, /device:TPU:2, one launch (start us, length us, event | category | flops | bytes accessed | tf_op | source)
XLA Modules:
  0.0 63.2 jit_solution(8093969537685420653)
XLA Ops:
  0.6 60.7 %distill_backward.1 = (f32[2,3584]{1,0:T(2,128)S(1)}, bf16[3584,512]{1,0:T(8,128)(2,1)S(1)}) custom-call(bf16[128,3584]{1,0:T(8,128)(2,1)} %hid.1, s32[1,128]{1,0:T(1,128)} %bitcast.3, s32[1,512]{1,0:T(1,128)} %bitcast.2, bf16[3584,512]{1,0:T(8,128)(2,1)} %w_hbm.1, bf16[128,4,512]{2,1,0:T(4,128)(2,1)} %t_hbm.1), custom_call_target="tpu_custom_call" | custom-call | tf_op jit(solution)/shard_map/distill_backward/pallas_call | solution.py:475
  61.3 1.9 %write_out.1 = (f32[2,3584]{1,0:T(2,128)}, bf16[3584,512]{1,0:T(8,128)(2,1)}) custom-call(f32[2,3584]{1,0:T(2,128)S(1)} %get-tuple-element.4.sums, bf16[3584,512]{1,0:T(8,128)(2,1)S(1)} %get-tuple-element.5.head), custom_call_target="tpu_custom_call" | custom-call | tf_op jit(solution)/shard_map/write_out/pallas_call | solution.py:539

commit v5 on v4

--- a/solution.py
+++ b/solution.py
@@ -137,6 +137,57 @@
     pair = [send(h_all.at[h, gi], h_all.at[h, gi], other) for h in range(2)]
     idc = [send(ids_all.at[gi], ids_all.at[gi], (lax.rem(gi + k, GRPS), vi)) for k in range(1, GRPS)]
 
+    gg = 2 * (1 - xh) + c
+    fwd_y, fwd_z = [], []
+
+    def forward(h):
+        cross_z[h].wait_recv()
+        piece = h_all.at[h, gg, :, zcols]
+        fwd_z.append([send(piece, piece, p) for p in zs])
+        cross_y[h].wait_recv()
+        piece = h_all.at[h, gg, :, ycols]
+        fwd_y.append([send(piece, piece, p) for p in ys])
+
+    def share(h):
+        cps = []
+        for fwd, cols in ((fwd_y, pl.ds(0, ZB)), (fwd_z, pl.ds(ZB, NZ * ZW))):
+            await_all(fwd[h])
+            piece = h_all.at[h, gg, :, cols]
+            cps.append(send(piece, piece, other))
+        return cps
+
+    def two_groups(part):
+        return pl.ds(pl.multiple_of(part * GROWS, GROWS), GROWS)
+
+    def logits(h, part):
+        a = h_all[h, pl.ds(2 * part, 2)].reshape(GROWS, DS)
+        lg[h, two_groups(part), :] = jnp.dot(a, w[...], preferred_element_type=F32)
+
+    def student_stats(h, part):
+        r = two_groups(part)
+        l = lg[h, r, :]
+        m = jnp.max(l, axis=1, keepdims=True)
+        e = jnp.exp((l - m) * 0.5)
+        lg[h, r, :] = e
+        lane = lax.broadcasted_iota(I32, (GROWS, 128), 1)
+        hard = jnp.sum(e * e, axis=1, keepdims=True)
+        soft = jnp.sum(e, axis=1, keepdims=True)
+        stc[h, r, :] = jnp.where(lane == 0, m, jnp.where(lane == 1, hard, soft))
+
+    def turn_rows(h, part):
+        cols = pl.ds(pl.multiple_of(h * HALF + part * GROWS, GROWS), GROWS)
+
+        def step(i, _):
+            s = pl.ds(pl.multiple_of(i * HW, HW), HW)
+            ht[s, cols] = h_all[h, pl.ds(2 * part, 2), :, s].reshape(GROWS, HW).T
+            return 0
+
+        lax.fori_loop(0, HCH, step, 0)
+
+    forward(0)
+    load_w.wait()
+    await_all(pair)
+    logits(0, xh)
     load_t.wait()
     for q in range(GRPS):
         tst[q] = tv[:, q, :]
@@ -147,58 +198,6 @@
     none = jnp.full((1, GROWS), -1e30, F32)
     for j in range(GRPS):
         sta[0, 3 + j // 2 : 4 + j // 2, (j % 2) * GROWS : (j % 2 + 1) * GROWS] = jnp.where(gi == j, lse, none)
-
-    gg = 2 * (1 - xh) + c
-    fwd_y, fwd_z = [], []
-
-    def forward(h):
-        cross_z[h].wait_recv()
-        piece = h_all.at[h, gg, :, zcols]
-        fwd_z.append([send(piece, piece, p) for p in zs])
-        cross_y[h].wait_recv()
-        piece = h_all.at[h, gg, :, ycols]
-        fwd_y.append([send(piece, piece, p) for p in ys])
-
-    def share(h):
-        cps = []
-        for fwd, cols in ((fwd_y, pl.ds(0, ZB)), (fwd_z, pl.ds(ZB, NZ * ZW))):
-            await_all(fwd[h])
-            piece = h_all.at[h, gg, :, cols]
-            cps.append(send(piece, piece, other))
-        return cps
-
-    def two_groups(part):
-        return pl.ds(pl.multiple_of(part * GROWS, GROWS), GROWS)
-
-    def logits(h, part):
-        a = h_all[h, pl.ds(2 * part, 2)].reshape(GROWS, DS)
-        lg[h, two_groups(part), :] = jnp.dot(a, w[...], preferred_element_type=F32)
-
-    def student_stats(h, part):
-        r = two_groups(part)
-        l = lg[h, r, :]
-        m = jnp.max(l, axis=1, keepdims=True)
-        e = jnp.exp((l - m) * 0.5)
-        lg[h, r, :] = e
-        lane = lax.broadcasted_iota(I32, (GROWS, 128), 1)
-        hard = jnp.sum(e * e, axis=1, keepdims=True)
-        soft = jnp.sum(e, axis=1, keepdims=True)
-        stc[h, r, :] = jnp.where(lane == 0, m, jnp.where(lane == 1, hard, soft))
-
-    def turn_rows(h, part):
-        cols = pl.ds(pl.multiple_of(h * HALF + part * GROWS, GROWS), GROWS)
-
-        def step(i, _):
-            s = pl.ds(pl.multiple_of(i * HW, HW), HW)
-            ht[s, cols] = h_all[h, pl.ds(2 * part, 2), :, s].reshape(GROWS, HW).T
-            return 0
-
-        lax.fori_loop(0, HCH, step, 0)
-
-    forward(0)
-    load_w.wait()
-    await_all(pair)
-    logits(0, xh)
     forward(1)
     teach = []
     for k in range(1, GRPS):
@@ -301,18 +300,25 @@
 
     first = (gi * (NX // 2 * NY * NZ) + vi) * COLS
 
+    def teacher_part(h):
+        def step(j, _):
+            full = pl.ds(pl.multiple_of(j * GROWS + h * HROWS, HROWS), HROWS)
+            f = rowt[full, :]
+            col = lax.broadcasted_iota(I32, (HROWS, COLS), 1) + first
+            hit = jnp.where(f[:, 0:1].astype(I32) == col, 16.0, 0.0)
+            al[full, :] = 32.0 * jnp.exp(al[full, :] * 0.5 - f[:, 1:2]) + hit
+            return 0
+
+        lax.fori_loop(0, GRPS, step, 0)
+
     def grad(h):
         def step(j, _):
             r = pl.ds(pl.multiple_of(j * HROWS, HROWS), HROWS)
             full = pl.ds(pl.multiple_of(j * GROWS + h * HROWS, HROWS), HROWS)
             f = fint[h, r, :]
-            f2 = rowt[full, :]
             e = lg[h, r, :]
-            col = lax.broadcasted_iota(I32, (HROWS, COLS), 1) + first
-            hit = jnp.where(f2[:, 0:1].astype(I32) == col, 16.0, 0.0)
-            soft = e * f[:, 0:1] - 32.0 * jnp.exp(al[full, :] * 0.5 - f2[:, 1:2])
             g[pl.ds(pl.multiple_of(h * HALF + j * HROWS, HROWS), HROWS), :] = (
-                soft + (e * e * f[:, 1:2] - hit)
+                e * (f[:, 0:1] + e * f[:, 1:2]) - al[full, :]
             ).astype(BF16)
             return 0
 
@@ -431,14 +437,16 @@
 
         lax.fori_loop(first, last, step, 0)
 
+    teacher_part(0)
     grad(0)
     m0 = pair_stage(0)
+    teacher_part(1)
     m0 = first_stage(0, m0)
     stats_end(1, m1)
     grad(1)
     m1 = pair_stage(1)
+    m1 = first_stage(1, m1)
     m0 = first_stage_end(0, m0)
-    m1 = first_stage(1, m1)
     for h in range(2):
         turn_rows(h, xh)
     m0 = second_stage(0, m0)

time: 64.2 us -> 63.7 us (level)
  no operation moved by 1% of the time
where the time goes in v5:
time: 63.7 us; the launch traced here: 63 us
  Pallas kernels  62.4 us (98%)
  between operations  0.64 us (1%)
    pallas_call x1, Pallas kernels, body(): pl.pallas_call(kernel, out_shape=(vm((2, DS), F32), vm((DS, COLS), BF16))...  60.5 us
    pallas_call x1, Pallas kernels, body(): pl.pallas_call(write_out, out_shape=(jax.ShapeDtypeStruct((2, DS), F32),...  1.91 us

profile of v5, /device:TPU:2, one launch (start us, length us, event | category | flops | bytes accessed | tf_op | source)
XLA Modules:
  0.0 63.0 jit_solution(12871476065280124978)
XLA Ops:
  0.6 60.5 %distill_backward.1 = (f32[2,3584]{1,0:T(2,128)S(1)}, bf16[3584,512]{1,0:T(8,128)(2,1)S(1)}) custom-call(bf16[128,3584]{1,0:T(8,128)(2,1)} %hid.1, s32[1,128]{1,0:T(1,128)} %bitcast.3, s32[1,512]{1,0:T(1,128)} %bitcast.2, bf16[3584,512]{1,0:T(8,128)(2,1)} %w_hbm.1, bf16[128,4,512]{2,1,0:T(4,128)(2,1)} %t_hbm.1), custom_call_target="tpu_custom_call" | custom-call | tf_op jit(solution)/shard_map/distill_backward/pallas_call | solution.py:483
  61.1 1.9 %write_out.1 = (f32[2,3584]{1,0:T(2,128)}, bf16[3584,512]{1,0:T(8,128)(2,1)}) custom-call(f32[2,3584]{1,0:T(2,128)S(1)} %get-tuple-element.4.sums, bf16[3584,512]{1,0:T(8,128)(2,1)S(1)} %get-tuple-element.5.head), custom_call_target="tpu_custom_call" | custom-call | tf_op jit(solution)/shard_map/write_out/pallas_call | solution.py:547

commit v6 on v5

--- a/solution.py
+++ b/solution.py
@@ -454,8 +454,8 @@
     for h in range(2):
         turn_rows(h, 1 - xh)
     head(0, 2)
+    m1 = second_stage(1, m1)
     third_stage(0, m0)
-    m1 = second_stage(1, m1)
     head(2, HCH)
     third_stage(1, m1)
     third_end()

time: 63.7 us -> 63.7 us (level)
  no operation moved by 1% of the time
where the time goes in v6:
time: 63.7 us; the launch traced here: 63.4 us
  Pallas kernels  62.8 us (99%)
  between operations  0.64 us (1%)
    pallas_call x1, Pallas kernels, body(): pl.pallas_call(kernel, out_shape=(vm((2, DS), F32), vm((DS, COLS), BF16))...  60.9 us
    pallas_call x1, Pallas kernels, body(): pl.pallas_call(write_out, out_shape=(jax.ShapeDtypeStruct((2, DS), F32),...  1.91 us

profile of v6, /device:TPU:2, one launch (start us, length us, event | category | flops | bytes accessed | tf_op | source)
XLA Modules:
  0.0 63.4 jit_solution(15737588003365772325)
XLA Ops:
  0.6 60.9 %distill_backward.1 = (f32[2,3584]{1,0:T(2,128)S(1)}, bf16[3584,512]{1,0:T(8,128)(2,1)S(1)}) custom-call(bf16[128,3584]{1,0:T(8,128)(2,1)} %hid.1, s32[1,128]{1,0:T(1,128)} %bitcast.3, s32[1,512]{1,0:T(1,128)} %bitcast.2, bf16[3584,512]{1,0:T(8,128)(2,1)} %w_hbm.1, bf16[128,4,512]{2,1,0:T(4,128)(2,1)} %t_hbm.1), custom_call_target="tpu_custom_call" | custom-call | tf_op jit(solution)/shard_map/distill_backward/pallas_call | solution.py:483
  61.5 1.9 %write_out.1 = (f32[2,3584]{1,0:T(2,128)}, bf16[3584,512]{1,0:T(8,128)(2,1)}) custom-call(f32[2,3584]{1,0:T(2,128)S(1)} %get-tuple-element.4.sums, bf16[3584,512]{1,0:T(8,128)(2,1)S(1)} %get-tuple-element.5.head), custom_call_target="tpu_custom_call" | custom-call | tf_op jit(solution)/shard_map/write_out/pallas_call | solution.py:547
